TPU v7x, 256 devices: a whole 4x4x8 slice. The times are simulated.
256 devices in a mesh: det: 32 (over z, y), sky: 8 (over x, core).
Axes of the slice: x: 4, y: 4, z: 8, core: 2. Of those that a mesh axis runs over, the one named last changes fastest.
Arguments:
- timelines: float32 [1024, 32768], P(('det', 'sky')), may hold values from -18 to 18
- knee_freq: float32 [1024], P(('det', 'sky')), may hold values from 1 to 100
- noise_slope: float32 [1024], P(('det', 'sky')), may hold values from 1 to 4
- noise_level: float32 [1024], P(('det', 'sky')), may hold values from 0.5 to 2
- templates: float32 [1024, 512], replicated, as said below
- interval_bounds: int32 [33], replicated, may hold values from 0 to 32768, as said below
- block_index: int32 [1024, 256], replicated, may hold values from 0 to 255
- block_slot: int32 [256], replicated, may hold values from 0 to 255, each once
Outputs:
- owned_map: float32 [256, 128], P('sky')
Inputs may be any that keep to these rules, and one draw needn't show every extreme that they name: interval_bounds starts at 0, ends at 32768 and rises strictly through multiples of 128; no interval is longer than 2048 samples, and in every draw one is exactly 2048 long. The columns of templates are orthonormal. Each row number appears once; sky index block_slot[b] // 32 owns block b.
All inputs are finite; a program needn't handle non-finite values.
Results may differ from a plain program's by a relative error of at most 0.000092.
Values sent between devices are 32-bit elements; how exact they have to be, the bound alone decides.
No kernel may reach another device: no remote copies, remote signals or barrier semaphores. Data moves between devices by JAX's collectives and lax.ppermute only.
A program may use at most 64 MiB of HBM per device.

v0:
```python
import math

import jax
import jax.numpy as jnp
from jax import lax
from jax.sharding import PartitionSpec as P

SEGLEN = 128


EPS = 1e-06


def phase_table(row_len, col_len, modulus):
    product = (
        jnp.arange(row_len, dtype=jnp.int32)[:, None]
        * jnp.arange(col_len, dtype=jnp.int32)[None, :]
        % modulus
    )
    angle = product.astype(jnp.float32) * (2.0 * math.pi / modulus)
    return (jnp.cos(angle), jnp.sin(angle))


def circulant_weight(timelines, knee_freq, noise_slope, noise_level):
    det_rows, length_all = timelines.shape
    outer_len = math.isqrt(length_all)
    while length_all % outer_len:
        outer_len -= 1
    inner_len = length_all // outer_len
    highest = lax.Precision.HIGHEST
    cos_outer, sin_outer = phase_table(outer_len, outer_len, outer_len)
    cos_inner, sin_inner = phase_table(inner_len, inner_len, inner_len)
    cos_twist, sin_twist = phase_table(outer_len, inner_len, length_all)
    folded = timelines.reshape(det_rows, outer_len, inner_len)
    section_re = jnp.einsum("kn,dnm->dkm", cos_outer, folded, precision=highest)
    section_im = -jnp.einsum("kn,dnm->dkm", sin_outer, folded, precision=highest)
    twist_re = section_re * cos_twist + section_im * sin_twist
    twist_im = section_im * cos_twist - section_re * sin_twist
    spec_re = jnp.einsum("dkm,ml->dkl", twist_re, cos_inner, precision=highest) + jnp.einsum(
        "dkm,ml->dkl", twist_im, sin_inner, precision=highest
    )
    spec_im = jnp.einsum("dkm,ml->dkl", twist_im, cos_inner, precision=highest) - jnp.einsum(
        "dkm,ml->dkl", twist_re, sin_inner, precision=highest
    )
    freq_index = (
        jnp.arange(outer_len, dtype=jnp.int32)[:, None]
        + outer_len * jnp.arange(inner_len, dtype=jnp.int32)[None, :]
    )
    fold = jnp.minimum(freq_index, length_all - freq_index).astype(jnp.float32)
    rising = jnp.power(fold[None, :, :], noise_slope[:, None, None])
    weight = (
        rising
        / (rising + jnp.power(knee_freq, noise_slope)[:, None, None])
        / (noise_level * noise_level)[:, None, None]
    )
    spec_re = spec_re * weight
    spec_im = spec_im * weight
    back_re = jnp.einsum("dkl,ml->dkm", spec_re, cos_inner, precision=highest) - jnp.einsum(
        "dkl,ml->dkm", spec_im, sin_inner, precision=highest
    )
    back_im = jnp.einsum("dkl,ml->dkm", spec_im, cos_inner, precision=highest) + jnp.einsum(
        "dkl,ml->dkm", spec_re, sin_inner, precision=highest
    )
    turn_re = back_re * cos_twist - back_im * sin_twist
    turn_im = back_im * cos_twist + back_re * sin_twist
    result = (
        jnp.einsum("nk,dkm->dnm", cos_outer, turn_re, precision=highest)
        - jnp.einsum("nk,dkm->dnm", sin_outer, turn_im, precision=highest)
    ) / length_all
    return result.reshape(det_rows, length_all)


def local(
    timelines,
    knee_freq,
    noise_slope,
    noise_level,
    templates,
    interval_bounds,
    block_index,
    block_slot,
):
    det_rows, samples = timelines.shape
    det_total = templates.shape[0]
    blocks = block_slot.shape[0]
    det_count = lax.axis_size("det")
    sky_count = lax.axis_size("sky")
    longest = 2 * samples // det_count
    highest = lax.Precision.HIGHEST
    weighted = circulant_weight(timelines, knee_freq, noise_slope, noise_level)
    interval = lax.axis_index("det")
    sub_index = lax.axis_index("sky")
    padded = jnp.concatenate([weighted, jnp.zeros((det_rows, longest), jnp.float32)], axis=1)

    def cut_piece(piece_start):
        return lax.dynamic_slice_in_dim(padded, piece_start, longest, 1)

    pieces = jax.vmap(cut_piece)(interval_bounds[:-1]).reshape(det_count, 1, det_rows, longest)
    sub_len = longest // sky_count
    seg_count = sub_len // SEGLEN
    regrouped = lax.all_to_all(
        lax.all_to_all(pieces, "det", split_axis=0, concat_axis=0, tiled=True),
        "sky",
        split_axis=3,
        concat_axis=1,
        tiled=True,
    )
    local_data = regrouped.reshape(det_total, sub_len)
    amplitudes = lax.dot_general(templates, local_data, (((0,), (0,)), ((), ())), precision=highest)
    cleaned = local_data - jnp.dot(templates, amplitudes, precision=highest)
    padded_index = jnp.concatenate(
        [block_index, jnp.zeros((det_total, longest // SEGLEN), jnp.int32)], axis=1
    )
    interval_len = interval_bounds[interval + 1] - interval_bounds[interval]
    in_interval = sub_index * sub_len + jnp.arange(sub_len, dtype=jnp.int32) < interval_len
    power_sum = jnp.sum(jnp.where(in_interval[None, :], cleaned * cleaned, 0.0), axis=1)
    total_power = lax.psum(power_sum, "sky")
    variance = total_power / interval_len.astype(jnp.float32) + EPS
    values = (cleaned / variance[:, None]).reshape(det_total * seg_count, SEGLEN)
    first_segment = (interval_bounds[interval] + sub_index * sub_len) // SEGLEN
    local_index = lax.dynamic_slice_in_dim(padded_index, first_segment, seg_count, 1)
    seg_inside = (
        sub_index * sub_len + jnp.arange(seg_count, dtype=jnp.int32) * SEGLEN < interval_len
    )
    slot_ids = jnp.where(seg_inside[None, :], jnp.take(block_slot, local_index), blocks).reshape(
        det_total * seg_count
    )
    owned_rows = blocks // sky_count
    map_scale = 1.0 / math.sqrt(det_total * samples // (SEGLEN * blocks))
    onehot = (slot_ids[None, :] == jnp.arange(blocks, dtype=jnp.int32)[:, None]).astype(jnp.float32)
    partial_map = jnp.dot(onehot, values, precision=highest)
    total_map = lax.psum(partial_map, ("det", "sky"))
    owned_map = lax.dynamic_slice_in_dim(total_map, sub_index * owned_rows, owned_rows, 0)
    return owned_map * map_scale


def solution(mesh):
    return jax.shard_map(
        local,
        mesh=mesh,
        in_specs=(
            P(("det", "sky"), None),
            P(("det", "sky")),
            P(("det", "sky")),
            P(("det", "sky")),
            P(),
            P(),
            P(),
            P(),
        ),
        out_specs=P("sky", None),
        check_vma=False,
    )
```

profile of v0, /device:TPU:1, one launch (start us, length us, event | category | flops | bytes accessed | tf_op | source)
XLA Modules:
  0.0 455.7 jit_solution(18444294333954852359)
XLA Ops:
  7.1 2.0 convolution_negate_fusion
  9.1 1.9 fusion.9
  11.1 2.4 fusion.15
  13.4 2.4 fusion.11
  15.9 3.1 fusion.5
  20.6 2.0 fusion.4
  22.7 1.7 fusion.33
  26.0 1.6 convolution_add_fusion
  30.7 62.7 %while.1 = (s32[]{:T(128)}, f32[4,34816]{1,0:T(4,128)S(1)}, s32[32,2]{0,1:T(2,128)S(1)}, f32[32,4,2048]{2,1,0:T(4,128)}, s32[]{:T(128)}) while((s32[]{:T(128)}, f32[4,34816]{1,0:T(4,128)S(1)}, s32[32,2]{0,1:T(2,128)S(1)}, f32[32,4,2048]{2,1,0:T(4,128)}, s32[]{:T(128)}) %tuple.19), condition=%wide.while_cond, body=%wide.while_body.sunk | while | flops 2 | bytes 66649 | solution.py:96
  93.4 38.2 %all_to_all.20 = f32[32,1,4,2048]{3,2,1,0:T(4,128)S(1)} all-to-all(f32[32,1,4,2048]{3,2,1,0:T(4,128)} %bitcast.86), channel_id=1, replica_groups=mesh['det'=32,'sky'=8] {'det'}, dimensions={0} | all-to-all | bytes 2097152 | tf_op jit(solution)/shard_map/all_to_all | solution.py:102
  131.7 3.1 copy.28
  134.8 5.3 %reshape.158 = f32[8,1,32768]{2,1,0:T(1,128)} reshape(f32[2048,1,4,32]{3,2,1,0:T(4,128)} %bitcast.79) | data formatting | bytes 2097152
  140.1 7.2 %all-to-all-start.1 = ((f32[8,1,32768]{2,1,0:T(1,128)}), f32[8,1,32768]{2,1,0:T(1,128)}, u32[]{:S(2)}, u32[]{:S(2)}) async-start(f32[8,1,32768]{2,1,0:T(1,128)} %reshape.158), calls=%async_computation.1 | async-start | bytes 2097152 | tf_op jit(solution)/shard_map/all_to_all | solution.py:101
  152.3 13.1 %gather_fusion = s32[2048]{0:T(1024)S(1)} fusion(s32[256]{0:T(256)S(1)} %copy-done.1, s32[2048]{0:T(1024)S(1)} %broadcast_clamp_fusion), kind=kCustom, calls=%fused_computation | custom fusion | bytes 24576 | tf_op jit(solution)/shard_map/jit(_take)/gather | solution.py:125
  166.8 2.1 select_select_fusion
  170.7 4.4 reduce
  175.1 4.1 reshape.159
  179.2 4.7 %copy.29 = f32[32,1,4,8,256]{4,2,3,0,1:T(4,128)} copy(f32[32,1,4,8,256]{0,2,4,3,1:T(4,128)} %bitcast.80) | data formatting | bytes 2097152 | tf_op jit(solution)/shard_map/all_to_all | solution.py:101
  183.8 1.6 reshape.123
  186.7 1.9 fusion.131
  188.7 3.0 select_reduce_fusion
  191.6 12.2 %psum.14 = f32[1024]{0:T(1024)S(1)} all-reduce(f32[1024]{0:T(1024)S(1)} %get-tuple-element.23), channel_id=1, replica_groups=mesh['det'=32,'sky'=8] {'sky'}, use_global_device_ids=true, to_apply=%region_1.2 | all-reduce | flops 1024 | bytes 8192 | tf_op jit(solution)/shard_map/psum | solution.py:117
  207.7 1.9 fusion
  209.6 237.9 %all-reduce.5.cloned.1.call-done = f32[256,128]{1,0:T(8,128)} async-done(((f32[256,128]{1,0:T(8,128)}), f32[256,128]{1,0:T(8,128)}) %all-reduce.5.cloned.1.call-update) | async-done | bytes 131088 | tf_op jit(solution)/shard_map/psum | solution.py:132
  (149 shorter events, 82.2 us)
Async XLA Ops:
  6.5 180.2 %copy-start = (f32[1024,512]{1,0:T(8,128)S(1)}, f32[1024,512]{1,0:T(8,128)}, u32[]{:S(2)}) copy-start(f32[1024,512]{1,0:T(8,128)} %param.12) | copy-start | bytes 6291460
  11.0 4.8 %copy-start.7 = (f32[4]{0:T(128)S(1)}, f32[4]{0:T(128)}, u32[]{:S(2)}) copy-start(f32[4]{0:T(128)} %param.11) | copy-start | bytes 52
  11.0 4.8 %copy-start.8 = (f32[4]{0:T(128)S(1)}, f32[4]{0:T(128)}, u32[]{:S(2)}) copy-start(f32[4]{0:T(128)} %param.9) | copy-start | bytes 52
  11.0 4.8 %copy-start.9 = (f32[4]{0:T(128)S(1)}, f32[4]{0:T(128)}, u32[]{:S(2)}) copy-start(f32[4]{0:T(128)} %param.10) | copy-start | bytes 52
  15.9 4.7 %copy-start.5 = (f32[4,128,256]{2,1,0:T(8,128)S(1)}, f32[4,128,256]{2,1,0:T(8,128)}, u32[]{:S(2)}) copy-start(f32[4,128,256]{2,1,0:T(8,128)} %fusion.11) | copy-start | bytes 1572868
  28.8 1.8 copy-start.6
  140.1 9.8 %copy-start.2 = (s32[1024,256]{1,0:T(8,128)S(1)}, s32[1024,256]{1,0:T(8,128)}, u32[]{:S(2)}) copy-start(s32[1024,256]{1,0:T(8,128)} %param.14) | copy-start | bytes 3145732
  140.1 12.2 %copy-start.1 = (s32[256]{0:T(256)S(1)}, s32[256]{0:T(256)}, u32[]{:S(2)}) copy-start(s32[256]{0:T(256)} %param.15) | copy-start | bytes 3076
  140.1 30.0 %all-to-all-start.1 = ((f32[8,1,32768]{2,1,0:T(1,128)}), f32[8,1,32768]{2,1,0:T(1,128)}, u32[]{:S(2)}, u32[]{:S(2)}) async-start(f32[8,1,32768]{2,1,0:T(1,128)} %reshape.158), calls=%async_computation.1 | async-start | bytes 2097152 | tf_op jit(solution)/shard_map/all_to_all | solution.py:101
  147.4 300.2 %all-reduce.5.cloned.1.call-start = ((), (), s32[]{:S(2)}) async-start(), calls=%async_computation.2 | async-start | bytes 262144 | tf_op jit(solution)/shard_map/psum | solution.py:132
  152.3 14.5 %copy-start.3 = (s32[1024,256]{1,0:T(8,128)S(1)}, s32[1024,256]{1,0:T(8,128)}, u32[]{:S(2)}) copy-start(s32[1024,256]{1,0:T(8,128)} %param.14) | copy-start | bytes 3145732
  186.7 1.9 copy-start.4
Sparse Core Ops, SparseCore 0:
  209.8 237.7 all-reduce.4
where the time goes:
time: 457 us; the launch traced here: 456 us
  waiting for transfers between devices  238 us (52%)
  local copies, waits for them, and re-layouts  104 us (23%)
  blocking collectives  50.4 us (11%)
  matrix products  29.4 us (6%)
  between operations  15.6 us (3%)
  other arithmetic  10.7 us (2%)
  starting transfers between devices  7.23 us (2%)
    psum x1, waiting for transfers between devices, local(): total_map = lax.psum(partial_map, ('det', 'sky'))  238 us
    gather x96, local copies, waits for them, and re-layouts  62.7 us
    all_to_all x1, blocking collectives, local(): lax.all_to_all(pieces, 'det', split_axis=0, concat_axis=0, tiled=True)  38.2 us
    gather x2, local copies, waits for them, and re-layouts, local(): jnp.take(block_slot, local_index)  14.4 us
    psum x1, blocking collectives, local(): total_power = lax.psum(power_sum, 'sky')  12.2 us
    unnamed x23, local copies, waits for them, and re-layouts  9.84 us
  transfers between devices with their start and end apart: 2, of which 1 were waited for; matrix products, arithmetic and copies ran while one was open for 5% of the time, Pallas kernels for 0%

commit v1 on v0

v1 whole, which is shorter than its diff:
```python
import math

import jax
import jax.numpy as jnp
import numpy as np
from jax import lax
from jax.experimental import pallas as pl
from jax.experimental.pallas import tpu as pltpu
from jax.sharding import Mesh, PartitionSpec as P

DETS = 1024
SAMPLES = 32768
TEMPLATES = 512
SEGLEN = 128
SEGMENTS = 256
BLOCKS = 256
INTERVALS = 32
EPS = 1e-06
OWN_DETS = 4
HALF = SEGMENTS // 2
ROWS = HALF + 8
GROUP = 16
GROUPS = SEGMENTS // GROUP
MAP_SCALE = 1.0 / math.sqrt(DETS * SAMPLES // (SEGLEN * BLOCKS))
ALL = ("z", "yh", "yl", "x", "c")
bf16 = jnp.bfloat16
f32 = jnp.float32


def split_np(table):
    high = np.asarray(table, np.float32).astype(jnp.bfloat16)
    low = (table - high.astype(np.float64)).astype(np.float32).astype(jnp.bfloat16)
    return high, low


def tables():
    k = np.arange(HALF)
    c = np.arange(SEGMENTS)
    angle = 2.0 * np.pi * ((k[:, None] * c[None, :]) % SEGMENTS) / SEGMENTS
    outer = np.concatenate([np.cos(angle), -np.sin(angle)], axis=0)
    outer[HALF] = 1.0 - 2.0 * (c % 2)
    p = np.arange(SEGLEN)
    angle = 2.0 * np.pi * ((p[:, None] * p[None, :]) % SEGLEN) / SEGLEN
    inner = np.block([[np.cos(angle), -np.sin(angle)], [np.sin(angle), np.cos(angle)]])
    row = np.arange(ROWS)
    angle = 2.0 * np.pi * (row[:, None] * p[None, :]) / SAMPLES
    freq = row[:, None] + SEGMENTS * p[None, :]
    fold = np.minimum(freq, SAMPLES - freq)
    log_fold = np.where(fold > 0, np.log(np.maximum(fold, 1)), 0.0)
    return (
        *split_np(outer),
        *split_np(inner),
        np.cos(angle).astype(np.float32),
        np.sin(angle).astype(np.float32),
        log_fold.astype(np.float32),
    )


def split(value):
    high = value.astype(bf16)
    return high, (value - high.astype(f32)).astype(bf16)


def dot3(a, b, dims):
    def one(x, y):
        return lax.dot_general(x, y, (dims, ((), ())), preferred_element_type=f32)

    return one(a[0], b[0]) + (one(a[0], b[1]) + one(a[1], b[0]))


NN = ((1,), (0,))
NT = ((1,), (1,))
TN = ((0,), (0,))


def group_at(block):
    z, yh = divmod(block, 2)
    return 2 * z + (yh ^ (z & 1))


def weight_kernel(
    knee_ref, slope_ref, level_ref, x_ref, fh_ref, fl_ref, mh_ref, ml_ref, cos_ref, sin_ref, log_ref, out_ref
):
    parts = [split(x_ref[pl.ds(d, SEGMENTS, stride=OWN_DETS), :]) for d in range(OWN_DETS)]
    outer = (fh_ref[...], fl_ref[...])
    inner = (mh_ref[...], ml_ref[...])
    cos, sin, log_fold = cos_ref[...], sin_ref[...], log_ref[...]
    samples = tuple(jnp.concatenate([part[i] for part in parts], axis=1) for i in range(2))
    section = dot3(outer, samples, NN)
    top = lax.broadcasted_iota(jnp.int32, (8, SEGLEN), 0) == 0
    stacked = []
    for d in range(OWN_DETS):
        cut = slice(SEGLEN * d, SEGLEN * (d + 1))
        real, imag = section[:HALF, cut], section[HALF:, cut]
        real = jnp.concatenate([real, jnp.where(top, imag[:8], 0.0)], axis=0)
        imag = jnp.concatenate([jnp.where(top, 0.0, imag[:8]), imag[8:], jnp.zeros((8, SEGLEN), f32)], axis=0)
        stacked.append(jnp.concatenate([real * cos + imag * sin, imag * cos - real * sin], axis=1))
    spectrum = dot3(split(jnp.concatenate(stacked, axis=0)), inner, NN)
    row = lax.broadcasted_iota(jnp.int32, (ROWS, SEGLEN), 0)
    zero_freq = (row == 0) & (lax.broadcasted_iota(jnp.int32, (ROWS, SEGLEN), 1) == 0)
    times = jnp.where((row == 0) | (row == HALF), 1.0 / SAMPLES, 2.0 / SAMPLES).astype(f32)
    shaped = []
    for d in range(OWN_DETS):
        log_knee = jnp.log(jnp.full((1, SEGLEN), knee_ref[d], f32))
        slope = slope_ref[d]
        level = jnp.full((1, SEGLEN), level_ref[d], f32)
        ratio = jnp.exp(slope * (log_knee - log_fold))
        weight = jnp.where(zero_freq, 0.0, times / ((1.0 + ratio) * (level * level)))
        part = spectrum[ROWS * d : ROWS * (d + 1)]
        shaped.append(part * jnp.concatenate([weight, weight], axis=1))
    back = dot3(split(jnp.concatenate(shaped, axis=0)), inner, NT)
    turned = []
    for d in range(OWN_DETS):
        part = back[ROWS * d : ROWS * (d + 1)]
        real, imag = part[:, :SEGLEN], part[:, SEGLEN:]
        turn_re = real * cos - imag * sin
        turn_im = imag * cos + real * sin
        first = jnp.where(top, jnp.broadcast_to(turn_re[HALF : HALF + 1], (8, SEGLEN)), turn_im[:8])
        turned.append(jnp.concatenate([turn_re[:HALF], first, turn_im[8:HALF]], axis=0))
    result = dot3(outer, split(jnp.concatenate(turned, axis=1)), TN)
    for d in range(OWN_DETS):
        for block in range(GROUPS):
            start = GROUP * group_at(block)
            out_ref[pl.ds(GROUP * OWN_DETS * block + d, GROUP, stride=OWN_DETS), :] = result[
                start : start + GROUP, SEGLEN * d : SEGLEN * (d + 1)
            ]


def project_kernel(data_ref, templates_ref, clean_ref, power_ref):
    data = data_ref[...].T
    pattern = split(templates_ref[...])
    amplitudes = dot3(split(data), pattern, NN)
    cleaned = data - dot3(split(amplitudes), pattern, NT)
    clean_ref[...] = cleaned
    power = jnp.sum(cleaned * cleaned, axis=0, keepdims=True)
    power = jnp.concatenate([power[:, SEGLEN * k : SEGLEN * (k + 1)] for k in range(8)], axis=0)
    for member in range(GROUP):
        power_ref[member] = power


def interval_of(bounds_ref, segment):
    at = segment * SEGLEN
    first = jnp.int32(0)
    end = jnp.int32(SAMPLES)
    for t in range(1, INTERVALS):
        bound = bounds_ref[t]
        first = jnp.where(bound <= at, jnp.maximum(first, bound), first)
        end = jnp.where(bound > at, jnp.minimum(end, bound), end)
    return first // SEGLEN, end // SEGLEN


def masked_sum(gathered_ref, base, first, end):
    total = jnp.zeros((8, SEGLEN), f32)
    for member in range(GROUP):
        inside = (base + member >= first) & (base + member < end)
        total = total + jnp.where(inside, 1.0, 0.0) * gathered_ref[member]
    return total


def halo_kernel(bounds_ref, segment_ref, gathered_ref, own_ref, ahead_ref, behind_ref):
    segment = segment_ref[0]
    base = segment // GROUP * GROUP
    first, end = interval_of(bounds_ref, segment)
    own_ref[...] = masked_sum(gathered_ref, base, first, end)
    first, end = interval_of(bounds_ref, base + GROUP)
    ahead_ref[...] = masked_sum(gathered_ref, base, first, end)
    first, end = interval_of(bounds_ref, base - 1)
    behind_ref[...] = masked_sum(gathered_ref, base, jnp.where(base == 0, end, first), end)


def slot_kernel(segment_ref, index_ref, slot_ref, hot_ref):
    segment = segment_ref[0]
    pick = lax.broadcasted_iota(jnp.int32, (8, SEGMENTS), 1) == segment
    index = index_ref[...].astype(f32).astype(bf16)
    seen = lax.dot_general(
        jnp.where(pick, 1.0, 0.0).astype(bf16), index, (NT, ((), ())), preferred_element_type=f32
    )
    block = lax.broadcasted_iota(jnp.int32, (BLOCKS, DETS), 0)
    hot = jnp.where(jnp.broadcast_to(seen[0:1].astype(jnp.int32), (BLOCKS, DETS)) == block, 1.0, 0.0).astype(bf16)
    table = jnp.broadcast_to(slot_ref[...].astype(f32).astype(bf16), (8, BLOCKS))
    slot = lax.dot_general(table, hot, (NN, ((), ())), preferred_element_type=f32)
    row = ((block >> 3) & 7) * 32 + (block >> 6) * 8 + (block & 7)
    hot_ref[...] = jnp.where(
        jnp.broadcast_to(slot[0:1].astype(jnp.int32), (BLOCKS, DETS)) == row, 1.0, 0.0
    ).astype(bf16)


def bin_kernel(bounds_ref, segment_ref, clean_ref, own_ref, before_ref, after_ref, hot_ref, map_ref):
    segment = segment_ref[0]
    base = segment // GROUP * GROUP
    first, end = interval_of(bounds_ref, segment)
    total = own_ref[...]
    total = total + jnp.where(first < base, 1.0, 0.0) * before_ref[...]
    total = total + jnp.where(end > base + GROUP, 1.0, 0.0) * after_ref[...]
    length = jnp.full((8, SEGLEN), (end - first) * SEGLEN, jnp.int32).astype(f32)
    inverse = 1.0 / (total / length + EPS)
    values = jnp.concatenate(
        [clean_ref[:, SEGLEN * k : SEGLEN * (k + 1)] * inverse[k : k + 1] for k in range(8)], axis=1
    )
    high, low = split(values)
    hot = hot_ref[...]
    map_ref[...] = lax.dot_general(hot, high, (NT, ((), ())), preferred_element_type=f32) + lax.dot_general(
        hot, low, (NT, ((), ())), preferred_element_type=f32
    )


def fold_kernel(parts_ref, out_ref):
    total = parts_ref[0]
    for i in range(1, parts_ref.shape[0]):
        total = total + parts_ref[i]
    total = total * MAP_SCALE
    for i in range(out_ref.shape[0]):
        out_ref[i] = total


VMEM = pl.BlockSpec(memory_space=pltpu.VMEM)
SMEM = pl.BlockSpec(memory_space=pltpu.SMEM)


def call(kernel, specs, outs, name):
    shapes = [jax.ShapeDtypeStruct(shape, dtype) for shape, dtype in outs]
    return pl.pallas_call(
        kernel,
        out_shape=shapes if len(shapes) > 1 else shapes[0],
        in_specs=specs,
        out_specs=[VMEM] * len(shapes) if len(shapes) > 1 else VMEM,
        compiler_params=pltpu.CompilerParams(vmem_limit_bytes=32 * 1024 * 1024),
        name=name,
    )


def neighbour_pairs():
    at = {group_at(block): block for block in range(GROUPS)}
    ahead = []
    for g in range(GROUPS - 1):
        (z, yh), (z_to, yh_to) = divmod(at[g], 2), divmod(at[g + 1], 2)
        for yl in range(2):
            yl_to = yl if yh == yh_to else 1 - yl
            ahead.append(((z * 2 + yh) * 2 + yl, (z_to * 2 + yh_to) * 2 + yl_to))
    return ahead, [(b, a) for a, b in ahead]


def local(timelines, knee_freq, noise_slope, noise_level, templates, interval_bounds, block_index, block_slot):
    z, yh = lax.axis_index("z"), lax.axis_index("yh")
    member = lax.axis_index(("yl", "x", "c"))
    segment = ((2 * z + (yh ^ (z & 1))) * GROUP + member).astype(jnp.int32).reshape(1)
    rows = timelines.reshape(OWN_DETS, SEGMENTS, SEGLEN).transpose(1, 0, 2).reshape(DETS, SEGLEN)
    weighted = call(weight_kernel, [SMEM] * 3 + [VMEM] * 8, [((DETS, SEGLEN), f32)], "weight")(
        knee_freq, noise_slope, noise_level, rows, *[jnp.asarray(t) for t in tables()]
    )
    data = lax.all_to_all(
        weighted.reshape(SEGMENTS, OWN_DETS, SEGLEN), ALL, split_axis=0, concat_axis=0, tiled=True
    ).reshape(DETS, SEGLEN)
    cleaned, power = call(
        project_kernel, [VMEM] * 2, [((SEGLEN, DETS), f32), ((GROUP, 8, SEGLEN), f32)], "project"
    )(data, templates)
    gathered = lax.all_to_all(power, ("yl", "x", "c"), split_axis=0, concat_axis=0, tiled=True)
    own, ahead, behind = call(halo_kernel, [SMEM] * 2 + [VMEM], [((8, SEGLEN), f32)] * 3, "halo")(
        interval_bounds, segment, gathered
    )
    up, down = neighbour_pairs()
    before = lax.ppermute(ahead, ("z", "yh", "yl"), up)
    after = lax.ppermute(behind, ("z", "yh", "yl"), down)
    hot = call(slot_kernel, [SMEM] + [VMEM] * 2, [((BLOCKS, DETS), bf16)], "slots")(
        segment, block_index, block_slot.reshape(1, BLOCKS)
    )
    partial = call(bin_kernel, [SMEM] * 2 + [VMEM] * 5, [((BLOCKS, SEGLEN), f32)], "bin")(
        interval_bounds, segment, cleaned, own, before, after, hot
    )
    spread = lax.all_to_all(
        partial.reshape(32, 8, SEGLEN), ("yh", "yl", "x", "c"), split_axis=0, concat_axis=0, tiled=True
    )
    copies = call(fold_kernel, [VMEM], [((32, 8, SEGLEN), f32)], "fold")(spread)
    sums = lax.all_to_all(copies, ("z", "yh", "yl"), split_axis=0, concat_axis=0, tiled=True)
    return jnp.sum(sums.reshape(8, 32, SEGLEN), axis=0)


def solution(mesh):
    whole = Mesh(mesh.devices.reshape(8, 2, 2, 4, 2), ALL)
    return jax.shard_map(
        local,
        mesh=whole,
        in_specs=(P(ALL, None), P(ALL), P(ALL), P(ALL), P(), P(), P(), P()),
        out_specs=P(("x", "c"), None),
        check_vma=False,
    )
```

time: 457 us -> 97.8 us (0.21)
  waiting for transfers between devices: 238 us -> 9.59 us
  local copies, waits for them, and re-layouts: 104 us -> 9.44 us
  matrix products: 29.4 us -> 0 us
  between operations: 15.6 us -> 0.11 us
  blocking collectives: 50.4 us -> 61.3 us
  other arithmetic: 10.7 us -> 0.62 us
  Pallas kernels: 0 us -> 7.21 us
    psum x1 -> x0, waiting for transfers between devices: 238 us -> none  [local(): total_map = lax.psum(partial_map, ('det', 'sky'))]
    gather x98 -> x0, local copies, waits for them, and re-layouts: 77.1 us -> none
    dot_general x15 -> x0, matrix products: 29.4 us -> none  [the longest x1 3.13 us: circulant_weight(): jnp.einsum('dkm,ml->dkl', twist_im, sin_inner, precision=highest)]
    all_to_all x1 -> x3, blocking collectives: 38.2 us -> 61.3 us  [the longest x1 35.4 us: local(): lax.all_to_all(weighted.reshape(SEGMENTS, OWN_DETS, SEGLEN), ALL, split_a...]
    psum x1 -> x0, blocking collectives: 12.2 us -> none  [local(): total_power = lax.psum(power_sum, 'sky')]
    all_to_all x3 -> x0, local copies, waits for them, and re-layouts: 8.29 us -> none  [the longest x2 5.17 us: local(): lax.all_to_all(lax.all_to_all(pieces, 'det', split_axis=0, concat_axis=0,...]
    pallas_call x0 -> x6, Pallas kernels: none -> 7.21 us  [the longest x1 2.4 us: local(): call(project_kernel, [VMEM] * 2, [((SEGLEN, DETS), f32), ((GROUP, 8, SEGL...]
    all_to_all x1, waiting for transfers between devices: 0.01 us -> 5.82 us  [local(): lax.all_to_all(power, ('yl', 'x', 'c'), split_axis=0, concat_axis=0, tile...]
  transfers between devices with their start and end apart: 2 -> 3, of which waited for: 1 -> 2; matrix products, arithmetic and copies ran while one was open for 5% -> 0% of each run, Pallas kernels for 0% -> 0%
where the time goes in v1:
time: 97.8 us; the launch traced here: 97.3 us
  blocking collectives  61.3 us (63%)
  waiting for transfers between devices  9.59 us (10%)
  local copies, waits for them, and re-layouts  9.44 us (10%)
  starting transfers between devices  9 us (9%)
  Pallas kernels  7.21 us (7%)
    all_to_all x1, blocking collectives, local(): lax.all_to_all(weighted.reshape(SEGMENTS, OWN_DETS, SEGLEN), ALL, split_a...  35.4 us
    all_to_all x1, blocking collectives, local(): lax.all_to_all(copies, ('z', 'yh', 'yl'), split_axis=0, concat_axis=0, ti...  13.8 us
    all_to_all x1, blocking collectives, local(): lax.all_to_all(partial.reshape(32, 8, SEGLEN), ('yh', 'yl', 'x', 'c'), sp...  12.2 us
    unnamed x30, local copies, waits for them, and re-layouts  9.44 us
    all_to_all x1, waiting for transfers between devices, local(): lax.all_to_all(power, ('yl', 'x', 'c'), split_axis=0, concat_axis=0, tile...  5.82 us
    all_to_all x1, starting transfers between devices, local(): lax.all_to_all(power, ('yl', 'x', 'c'), split_axis=0, concat_axis=0, tile...  4.83 us
    ppermute x1, waiting for transfers between devices, local(): after = lax.ppermute(behind, ('z', 'yh', 'yl'), down)  3.76 us
    ppermute x1, starting transfers between devices, local(): before = lax.ppermute(ahead, ('z', 'yh', 'yl'), up)  2.89 us
  transfers between devices with their start and end apart: 3, of which 2 were waited for; matrix products, arithmetic and copies ran while one was open for 0% of the time, Pallas kernels for 0%

profile of v1, /device:TPU:1, one launch (start us, length us, event | category | flops | bytes accessed | tf_op | source)
XLA Modules:
  0.0 97.3 jit_solution(13768070388500480226)
XLA Ops:
  0.0 1.2 %copy-done.2 = f32[4,32768]{1,0:T(4,128)S(1)} copy-done((f32[4,32768]{1,0:T(4,128)S(1)}, f32[4,32768]{1,0:T(4,128)}, u32[]{:S(2)}) %copy-start.2) | copy-done | bytes 524312
  1.2 0.9 copy-done.3
  2.1 0.9 copy-done.4
  3.0 0.9 copy-done.5
  3.9 0.9 copy-done.6
  4.8 0.9 copy-done.7
  5.7 0.9 copy-done.8
  6.6 0.9 copy-done.9
  7.5 0.7 copy-done.12
  8.1 0.7 copy-done.13
  8.8 0.7 copy-done.14
  9.4 2.3 %weight.1 = f32[1024,128]{1,0:T(8,128)S(1)} custom-call(f32[4]{0:T(128)S(1)} %copy-done.12, f32[4]{0:T(128)S(1)} %copy-done.13, f32[4]{0:T(128)S(1)} %copy-done.14, f32[1024,128]{1,0:T(8,128)S(1)} %bitcast.15, bf16[256,256]{1,0:T(8,128)(2,1)S(1)} %copy-done.6, bf16[256,256]{1,0:T(8,128)(2,1)S(1)} %copy-done.5, bf16[256,256]{1,0:T(8,128)(2,1)S(1)} %copy-done.4, ...), custom_call_target="tpu_custom_call" | custom-call | tf_op jit(solution)/shard_map/weight/pallas_call | solution.py:248
  11.8 35.4 %all_to_all.20 = f32[256,4,128]{2,1,0:T(4,128)S(1)} all-to-all(f32[256,4,128]{2,1,0:T(4,128)S(1)} %bitcast.13), channel_id=1, replica_groups=mesh['z'=8,'yh'=2,'yl'=2,'x'=4,'c'=2] {'z','yh','yl','x','c'}, dimensions={0} | all-to-all | bytes 1048576 | tf_op jit(solution)/shard_map/all_to_all | solution.py:251
  47.1 2.4 %project.1 = (f32[128,1024]{1,0:T(8,128)S(1)}, f32[16,8,128]{2,1,0:T(8,128)}) custom-call(f32[1024,128]{1,0:T(8,128)S(1)} %bitcast.14, f32[1024,512]{1,0:T(8,128)S(1)} %copy-done), custom_call_target="tpu_custom_call" | custom-call | tf_op jit(solution)/shard_map/project/pallas_call | solution.py:254
  49.5 4.8 %all-to-all-start.1 = ((f32[16,8,128]{2,1,0:T(8,128)}), f32[16,8,128]{2,1,0:T(8,128)S(1)}, u32[]{:S(2)}, u32[]{:S(2)}) async-start(f32[16,8,128]{2,1,0:T(8,128)} %get-tuple-element.11), calls=%async_computation.1 | async-start | bytes 131072 | tf_op jit(solution)/shard_map/all_to_all | solution.py:257
  54.3 5.8 %all-to-all-done.1.gathered_ref = f32[16,8,128]{2,1,0:T(8,128)S(1)} async-done(((f32[16,8,128]{2,1,0:T(8,128)}), f32[16,8,128]{2,1,0:T(8,128)S(1)}, u32[]{:S(2)}, u32[]{:S(2)}) %all-to-all-start.1) | async-done | bytes 65568 | tf_op jit(solution)/shard_map/all_to_all | solution.py:257
  60.2 0.9 halo.1
  61.1 2.9 %collective-permute-start = (f32[8,128]{1,0:T(8,128)S(1)}, f32[8,128]{1,0:T(8,128)S(1)}, u32[]{:S(2)}, u32[]{:S(2)}) collective-permute-start(f32[8,128]{1,0:T(8,128)S(1)} %get-tuple-element.13), channel_id=1, source_target_pairs={{0,24},{8,16},{16,48},{24,56},{48,40},{56,32},{32,64},{40,72},{64,... | collective-permute-start | bytes 12296 | tf_op jit(solution)/shard_map/ppermute | solution.py:262
  64.0 1.3 %collective-permute-start.1 = (f32[8,128]{1,0:T(8,128)S(1)}, f32[8,128]{1,0:T(8,128)S(1)}, u32[]{:S(2)}, u32[]{:S(2)}) collective-permute-start(f32[8,128]{1,0:T(8,128)S(1)} %get-tuple-element.14), channel_id=1, source_target_pairs={{24,0},{16,8},{48,16},{56,24},{40,48},{32,56},{64,32},{72,40},{88,... | collective-permute-start | bytes 12296 | tf_op jit(solution)/shard_map/ppermute | solution.py:263
  65.8 3.8 %collective-permute-done.1.after_ref = f32[8,128]{1,0:T(8,128)S(1)} collective-permute-done((f32[8,128]{1,0:T(8,128)S(1)}, f32[8,128]{1,0:T(8,128)S(1)}, u32[]{:S(2)}, u32[]{:S(2)}) %collective-permute-start.1) | collective-permute-done | bytes 4128 | tf_op jit(solution)/shard_map/ppermute | solution.py:263
  69.6 1.1 %bin.1 = f32[256,128]{1,0:T(8,128)S(1)} custom-call(s32[33]{0:T(128)S(1)} %copy-done.10, s32[1]{0:T(128)} %bitcast.segment_ref, f32[128,1024]{1,0:T(8,128)S(1)} %get-tuple-element.10.clean_ref, f32[8,128]{1,0:T(8,128)S(1)} %get-tuple-element.12.own_ref, f32[8,128]{1,0:T(8,128)S(1)} %collective-permute-done.before_ref, ...), custom_call_target="tpu_custom_call" | custom-call | tf_op jit(solution)/shard_map/bin/pallas_call | solution.py:267
  70.7 12.2 %all_to_all.21.parts_ref = f32[32,8,128]{2,1,0:T(8,128)S(1)} all-to-all(f32[32,8,128]{2,1,0:T(8,128)S(1)} %bitcast.16), channel_id=1, replica_groups=mesh['z'=8,'yh'=2,'yl'=2,'x'=4,'c'=2] {'yh','yl','x','c'}, dimensions={0} | all-to-all | bytes 262144 | tf_op jit(solution)/shard_map/all_to_all | solution.py:270
  82.9 13.8 %all_to_all.22 = f32[32,8,128]{2,1,0:T(8,128)S(1)} all-to-all(f32[32,8,128]{2,1,0:T(8,128)S(1)} %fold.1), channel_id=1, replica_groups=mesh['z'=8,'yh'=2,'yl'=2,'x'=4,'c'=2] {'z','yh','yl'}, dimensions={0} | all-to-all | bytes 262144 | tf_op jit(solution)/shard_map/all_to_all | solution.py:274
  96.7 0.6 bitcast_reduce_fusion
  (22 shorter events, 0.5 us)
Async XLA Ops:
  0.0 47.1 %copy-start = (f32[1024,512]{1,0:T(8,128)S(1)}, f32[1024,512]{1,0:T(8,128)}, u32[]{:S(2)}) copy-start(f32[1024,512]{1,0:T(8,128)} %templates_ref.1) | copy-start | bytes 6291460
  0.0 1.2 %copy-start.2 = (f32[4,32768]{1,0:T(4,128)S(1)}, f32[4,32768]{1,0:T(4,128)}, u32[]{:S(2)}) copy-start(f32[4,32768]{1,0:T(4,128)} %param.15) | copy-start | bytes 1572868
  1.2 0.9 copy-start.3
  2.1 0.9 copy-start.4
  3.0 0.9 copy-start.5
  3.9 0.9 copy-start.6
  4.8 0.9 copy-start.7
  5.7 0.9 copy-start.8
  6.6 0.9 copy-start.9
  7.5 0.7 copy-start.12
  8.1 0.7 copy-start.13
  8.8 0.7 copy-start.14
  11.7 48.4 %copy-start.10 = (s32[33]{0:T(128)S(1)}, s32[33]{0:T(128)}, u32[]{:S(2)}) copy-start(s32[33]{0:T(128)} %bounds_ref.3) | copy-start | bytes 400
  11.7 53.6 %copy-start.1 = (s32[1024,256]{1,0:T(8,128)S(1)}, s32[1024,256]{1,0:T(8,128)}, u32[]{:S(2)}) copy-start(s32[1024,256]{1,0:T(8,128)} %index_ref.1) | copy-start | bytes 3145732
  11.7 53.6 %copy-start.11 = (s32[256]{0:T(256)S(1)}, s32[256]{0:T(256)}, u32[]{:S(2)}) copy-start(s32[256]{0:T(256)} %param.22) | copy-start | bytes 3076
  49.5 10.7 %all-to-all-start.1 = ((f32[16,8,128]{2,1,0:T(8,128)}), f32[16,8,128]{2,1,0:T(8,128)S(1)}, u32[]{:S(2)}, u32[]{:S(2)}) async-start(f32[16,8,128]{2,1,0:T(8,128)} %get-tuple-element.11), calls=%async_computation.1 | async-start | bytes 131072 | tf_op jit(solution)/shard_map/all_to_all | solution.py:257
  61.1 4.7 %collective-permute-start = (f32[8,128]{1,0:T(8,128)S(1)}, f32[8,128]{1,0:T(8,128)S(1)}, u32[]{:S(2)}, u32[]{:S(2)}) collective-permute-start(f32[8,128]{1,0:T(8,128)S(1)} %get-tuple-element.13), channel_id=1, source_target_pairs={{0,24},{8,16},{16,48},{24,56},{48,40},{56,32},{32,64},{40,72},{64,... | collective-permute-start | bytes 12296 | tf_op jit(solution)/shard_map/ppermute | solution.py:262
  64.0 5.6 %collective-permute-start.1 = (f32[8,128]{1,0:T(8,128)S(1)}, f32[8,128]{1,0:T(8,128)S(1)}, u32[]{:S(2)}, u32[]{:S(2)}) collective-permute-start(f32[8,128]{1,0:T(8,128)S(1)} %get-tuple-element.14), channel_id=1, source_target_pairs={{24,0},{16,8},{48,16},{56,24},{40,48},{32,56},{64,32},{72,40},{88,... | collective-permute-start | bytes 12296 | tf_op jit(solution)/shard_map/ppermute | solution.py:263

commit v2 on v1

--- a/solution.py
+++ b/solution.py
@@ -21,6 +21,7 @@
 ROWS = HALF + 8
 GROUP = 16
 GROUPS = SEGMENTS // GROUP
+PLANE = 2 * GROUP
 MAP_SCALE = 1.0 / math.sqrt(DETS * SAMPLES // (SEGLEN * BLOCKS))
 ALL = ("z", "yh", "yl", "x", "c")
 bf16 = jnp.bfloat16
@@ -48,11 +49,8 @@
     fold = np.minimum(freq, SAMPLES - freq)
     log_fold = np.where(fold > 0, np.log(np.maximum(fold, 1)), 0.0)
     return (
-        *split_np(outer),
-        *split_np(inner),
-        np.cos(angle).astype(np.float32),
-        np.sin(angle).astype(np.float32),
-        log_fold.astype(np.float32),
+        np.stack([*split_np(outer), *split_np(inner)]),
+        np.stack([np.cos(angle), np.sin(angle), log_fold]).astype(np.float32),
     )
 
 
@@ -79,12 +77,26 @@
 
 
 def weight_kernel(
-    knee_ref, slope_ref, level_ref, x_ref, fh_ref, fl_ref, mh_ref, ml_ref, cos_ref, sin_ref, log_ref, out_ref
+    knee_hbm, slope_hbm, level_hbm, x_hbm, tables_hbm, factors_hbm, out_ref,
+    knee_ref, slope_ref, level_ref, x_ref, tables_ref, factors_ref, sems,
 ):
+    pairs = [
+        (x_hbm, x_ref),
+        (tables_hbm, tables_ref),
+        (factors_hbm, factors_ref),
+        (knee_hbm, knee_ref),
+        (slope_hbm, slope_ref),
+        (level_hbm, level_ref),
+    ]
+    copies = [pltpu.make_async_copy(src, dst, sems.at[i]) for i, (src, dst) in enumerate(pairs)]
+    for copy in copies:
+        copy.start()
+    for copy in copies:
+        copy.wait()
     parts = [split(x_ref[pl.ds(d, SEGMENTS, stride=OWN_DETS), :]) for d in range(OWN_DETS)]
-    outer = (fh_ref[...], fl_ref[...])
-    inner = (mh_ref[...], ml_ref[...])
-    cos, sin, log_fold = cos_ref[...], sin_ref[...], log_ref[...]
+    outer = (tables_ref[0], tables_ref[1])
+    inner = (tables_ref[2], tables_ref[3])
+    cos, sin, log_fold = factors_ref[0], factors_ref[1], factors_ref[2]
     samples = tuple(jnp.concatenate([part[i] for part in parts], axis=1) for i in range(2))
     section = dot3(outer, samples, NN)
     top = lax.broadcasted_iota(jnp.int32, (8, SEGLEN), 0) == 0
@@ -126,6 +138,22 @@
             ]
 
 
+def slot_kernel(segment_ref, index_ref, slot_ref, hot_ref):
+    pick = lax.broadcasted_iota(jnp.int32, (8, SEGMENTS), 1) == segment_ref[0]
+    index = index_ref[...].astype(f32).astype(bf16)
+    seen = lax.dot_general(
+        jnp.where(pick, 1.0, 0.0).astype(bf16), index, (NT, ((), ())), preferred_element_type=f32
+    )
+    block = lax.broadcasted_iota(jnp.int32, (BLOCKS, DETS), 0)
+    hot = jnp.where(jnp.broadcast_to(seen[0:1].astype(jnp.int32), (BLOCKS, DETS)) == block, 1.0, 0.0).astype(bf16)
+    table = jnp.broadcast_to(slot_ref[...].astype(f32).astype(bf16), (8, BLOCKS))
+    slot = lax.dot_general(table, hot, (NN, ((), ())), preferred_element_type=f32)
+    row = ((block >> 3) & 7) * 32 + (block >> 6) * 8 + (block & 7)
+    hot_ref[...] = jnp.where(
+        jnp.broadcast_to(slot[0:1].astype(jnp.int32), (BLOCKS, DETS)) == row, 1.0, 0.0
+    ).astype(bf16)
+
+
 def project_kernel(data_ref, templates_ref, clean_ref, power_ref):
     data = data_ref[...].T
     pattern = split(templates_ref[...])
@@ -134,7 +162,7 @@
     clean_ref[...] = cleaned
     power = jnp.sum(cleaned * cleaned, axis=0, keepdims=True)
     power = jnp.concatenate([power[:, SEGLEN * k : SEGLEN * (k + 1)] for k in range(8)], axis=0)
-    for member in range(GROUP):
+    for member in range(PLANE):
         power_ref[member] = power
 
 
@@ -149,51 +177,33 @@
     return first // SEGLEN, end // SEGLEN
 
 
-def masked_sum(gathered_ref, base, first, end):
+def masked_sum(gathered_ref, base, turn, first, end):
     total = jnp.zeros((8, SEGLEN), f32)
-    for member in range(GROUP):
-        inside = (base + member >= first) & (base + member < end)
+    for member in range(PLANE):
+        at = base + (member ^ turn)
+        inside = (at >= first) & (at < end)
         total = total + jnp.where(inside, 1.0, 0.0) * gathered_ref[member]
     return total
 
 
-def halo_kernel(bounds_ref, segment_ref, gathered_ref, own_ref, ahead_ref, behind_ref):
+def halo_kernel(bounds_ref, segment_ref, gathered_ref, own_ref, share_ref, message_ref):
     segment = segment_ref[0]
-    base = segment // GROUP * GROUP
+    plane = segment // PLANE
+    base = plane * PLANE
+    turn = (plane & 1) * GROUP
+    late = (segment & GROUP) != 0
     first, end = interval_of(bounds_ref, segment)
-    own_ref[...] = masked_sum(gathered_ref, base, first, end)
-    first, end = interval_of(bounds_ref, base + GROUP)
-    ahead_ref[...] = masked_sum(gathered_ref, base, first, end)
-    first, end = interval_of(bounds_ref, base - 1)
-    behind_ref[...] = masked_sum(gathered_ref, base, jnp.where(base == 0, end, first), end)
-
-
-def slot_kernel(segment_ref, index_ref, slot_ref, hot_ref):
-    segment = segment_ref[0]
-    pick = lax.broadcasted_iota(jnp.int32, (8, SEGMENTS), 1) == segment
-    index = index_ref[...].astype(f32).astype(bf16)
-    seen = lax.dot_general(
-        jnp.where(pick, 1.0, 0.0).astype(bf16), index, (NT, ((), ())), preferred_element_type=f32
-    )
-    block = lax.broadcasted_iota(jnp.int32, (BLOCKS, DETS), 0)
-    hot = jnp.where(jnp.broadcast_to(seen[0:1].astype(jnp.int32), (BLOCKS, DETS)) == block, 1.0, 0.0).astype(bf16)
-    table = jnp.broadcast_to(slot_ref[...].astype(f32).astype(bf16), (8, BLOCKS))
-    slot = lax.dot_general(table, hot, (NN, ((), ())), preferred_element_type=f32)
-    row = ((block >> 3) & 7) * 32 + (block >> 6) * 8 + (block & 7)
-    hot_ref[...] = jnp.where(
-        jnp.broadcast_to(slot[0:1].astype(jnp.int32), (BLOCKS, DETS)) == row, 1.0, 0.0
-    ).astype(bf16)
-
-
-def bin_kernel(bounds_ref, segment_ref, clean_ref, own_ref, before_ref, after_ref, hot_ref, map_ref):
-    segment = segment_ref[0]
-    base = segment // GROUP * GROUP
-    first, end = interval_of(bounds_ref, segment)
-    total = own_ref[...]
-    total = total + jnp.where(first < base, 1.0, 0.0) * before_ref[...]
-    total = total + jnp.where(end > base + GROUP, 1.0, 0.0) * after_ref[...]
     length = jnp.full((8, SEGLEN), (end - first) * SEGLEN, jnp.int32).astype(f32)
-    inverse = 1.0 / (total / length + EPS)
+    own_ref[...] = masked_sum(gathered_ref, base, turn, first, end) / length + EPS
+    beyond = jnp.where(late, end > base + PLANE, first < base)
+    share_ref[...] = jnp.where(beyond, 1.0, 0.0) / length
+    first, end = interval_of(bounds_ref, jnp.where(late, base + PLANE, base - 1))
+    edge = jnp.where(late, base + PLANE == SEGMENTS, base == 0)
+    message_ref[...] = masked_sum(gathered_ref, base, turn, jnp.where(edge, end, first), end)
+
+
+def bin_kernel(clean_ref, own_ref, share_ref, message_ref, hot_ref, map_ref):
+    inverse = 1.0 / (own_ref[...] + share_ref[...] * message_ref[...])
     values = jnp.concatenate(
         [clean_ref[:, SEGLEN * k : SEGLEN * (k + 1)] * inverse[k : k + 1] for k in range(8)], axis=1
     )
@@ -215,29 +225,29 @@
 
 VMEM = pl.BlockSpec(memory_space=pltpu.VMEM)
 SMEM = pl.BlockSpec(memory_space=pltpu.SMEM)
-
-
-def call(kernel, specs, outs, name):
+HBM = pl.BlockSpec(memory_space=pltpu.HBM)
+
+
+def call(kernel, specs, outs, name, scratch=(), mib=16):
     shapes = [jax.ShapeDtypeStruct(shape, dtype) for shape, dtype in outs]
     return pl.pallas_call(
         kernel,
         out_shape=shapes if len(shapes) > 1 else shapes[0],
         in_specs=specs,
         out_specs=[VMEM] * len(shapes) if len(shapes) > 1 else VMEM,
-        compiler_params=pltpu.CompilerParams(vmem_limit_bytes=32 * 1024 * 1024),
+        scratch_shapes=list(scratch),
+        compiler_params=pltpu.CompilerParams(vmem_limit_bytes=mib * 1024 * 1024),
         name=name,
     )
 
 
-def neighbour_pairs():
-    at = {group_at(block): block for block in range(GROUPS)}
-    ahead = []
-    for g in range(GROUPS - 1):
-        (z, yh), (z_to, yh_to) = divmod(at[g], 2), divmod(at[g + 1], 2)
-        for yl in range(2):
-            yl_to = yl if yh == yh_to else 1 - yl
-            ahead.append(((z * 2 + yh) * 2 + yl, (z_to * 2 + yh_to) * 2 + yl_to))
-    return ahead, [(b, a) for a, b in ahead]
+def swap_pairs():
+    pairs = []
+    for z in range(8):
+        for yh in range(2):
+            z_to = z ^ 1 if yh else (z + (1 if z % 2 else -1)) % 8
+            pairs.append((2 * z + yh, 2 * z_to + yh))
+    return pairs
 
 
 def local(timelines, knee_freq, noise_slope, noise_level, templates, interval_bounds, block_index, block_slot):
@@ -245,28 +255,30 @@
     member = lax.axis_index(("yl", "x", "c"))
     segment = ((2 * z + (yh ^ (z & 1))) * GROUP + member).astype(jnp.int32).reshape(1)
     rows = timelines.reshape(OWN_DETS, SEGMENTS, SEGLEN).transpose(1, 0, 2).reshape(DETS, SEGLEN)
-    weighted = call(weight_kernel, [SMEM] * 3 + [VMEM] * 8, [((DETS, SEGLEN), f32)], "weight")(
+    scratch = [pltpu.SMEM((OWN_DETS,), f32)] * 3 + [
+        pltpu.VMEM((DETS, SEGLEN), f32),
+        pltpu.VMEM((4, SEGMENTS, SEGMENTS), bf16),
+        pltpu.VMEM((3, ROWS, SEGLEN), f32),
+        pltpu.SemaphoreType.DMA((6,)),
+    ]
+    weighted = call(weight_kernel, [HBM] * 6, [((DETS, SEGLEN), f32)], "weight", scratch, 60)(
         knee_freq, noise_slope, noise_level, rows, *[jnp.asarray(t) for t in tables()]
     )
     data = lax.all_to_all(
         weighted.reshape(SEGMENTS, OWN_DETS, SEGLEN), ALL, split_axis=0, concat_axis=0, tiled=True
     ).reshape(DETS, SEGLEN)
-    cleaned, power = call(
-        project_kernel, [VMEM] * 2, [((SEGLEN, DETS), f32), ((GROUP, 8, SEGLEN), f32)], "project"
-    )(data, templates)
-    gathered = lax.all_to_all(power, ("yl", "x", "c"), split_axis=0, concat_axis=0, tiled=True)
-    own, ahead, behind = call(halo_kernel, [SMEM] * 2 + [VMEM], [((8, SEGLEN), f32)] * 3, "halo")(
-        interval_bounds, segment, gathered
-    )
-    up, down = neighbour_pairs()
-    before = lax.ppermute(ahead, ("z", "yh", "yl"), up)
-    after = lax.ppermute(behind, ("z", "yh", "yl"), down)
     hot = call(slot_kernel, [SMEM] + [VMEM] * 2, [((BLOCKS, DETS), bf16)], "slots")(
         segment, block_index, block_slot.reshape(1, BLOCKS)
     )
-    partial = call(bin_kernel, [SMEM] * 2 + [VMEM] * 5, [((BLOCKS, SEGLEN), f32)], "bin")(
-        interval_bounds, segment, cleaned, own, before, after, hot
-    )
+    cleaned, power = call(
+        project_kernel, [VMEM] * 2, [((SEGLEN, DETS), f32), ((PLANE, 8, SEGLEN), f32)], "project"
+    )(data, templates)
+    gathered = lax.all_to_all(power, ("yh", "yl", "x", "c"), split_axis=0, concat_axis=0, tiled=True)
+    own, share, message = call(halo_kernel, [SMEM] * 2 + [VMEM], [((8, SEGLEN), f32)] * 3, "halo")(
+        interval_bounds, segment, gathered
+    )
+    beyond = lax.ppermute(message, ("z", "yh"), swap_pairs())
+    partial = call(bin_kernel, [VMEM] * 5, [((BLOCKS, SEGLEN), f32)], "bin")(cleaned, own, share, beyond, hot)
     spread = lax.all_to_all(
         partial.reshape(32, 8, SEGLEN), ("yh", "yl", "x", "c"), split_axis=0, concat_axis=0, tiled=True
     )

time: 97.8 us -> 85.5 us (0.87)
  local copies, waits for them, and re-layouts: 9.44 us -> 0.02 us
  starting transfers between devices: 9 us -> 6.23 us
  Pallas kernels: 7.21 us -> 8.19 us
    unnamed x30 -> x8, local copies, waits for them, and re-layouts: 9.44 us -> 0.02 us
    ppermute x2 -> x1, starting transfers between devices: 4.18 us -> 1.23 us  [local(): beyond = lax.ppermute(message, ('z', 'yh'), swap_pairs())]
    all_to_all x1, waiting for transfers between devices: 5.82 us -> 7.61 us  [local(): lax.all_to_all(power, ('yh', 'yl', 'x', 'c'), split_axis=0, concat_axis=0...]
    ppermute x2 -> x1, waiting for transfers between devices: 3.77 us -> 2.05 us  [local(): beyond = lax.ppermute(message, ('z', 'yh'), swap_pairs())]
    pallas_call x3, Pallas kernels: 5.78 us -> 6.82 us  [the longest x1 3.98 us: local(): call(weight_kernel, [HBM] * 6, [((DETS, SEGLEN), f32)], 'weight', scratch...]
  transfers between devices with their start and end apart: 3 -> 2, of which waited for: 2 -> 2; matrix products, arithmetic and copies ran while one was open for 0% -> 0% of each run, Pallas kernels for 0% -> 1%
where the time goes in v2:
time: 85.5 us; the launch traced here: 85.2 us
  blocking collectives  60.4 us (71%)
  waiting for transfers between devices  9.66 us (11%)
  Pallas kernels  8.19 us (10%)
  starting transfers between devices  6.23 us (7%)
    all_to_all x1, blocking collectives, local(): lax.all_to_all(weighted.reshape(SEGMENTS, OWN_DETS, SEGLEN), ALL, split_a...  35.6 us
    all_to_all x1, blocking collectives, local(): lax.all_to_all(copies, ('z', 'yh', 'yl'), split_axis=0, concat_axis=0, ti...  12.9 us
    all_to_all x1, blocking collectives, local(): lax.all_to_all(partial.reshape(32, 8, SEGLEN), ('yh', 'yl', 'x', 'c'), sp...  11.9 us
    all_to_all x1, waiting for transfers between devices, local(): lax.all_to_all(power, ('yh', 'yl', 'x', 'c'), split_axis=0, concat_axis=0...  7.61 us
    all_to_all x1, starting transfers between devices, local(): lax.all_to_all(power, ('yh', 'yl', 'x', 'c'), split_axis=0, concat_axis=0...  5 us
    pallas_call x1, Pallas kernels, local(): call(weight_kernel, [HBM] * 6, [((DETS, SEGLEN), f32)], 'weight', scratch...  3.98 us
    pallas_call x1, Pallas kernels, local(): call(project_kernel, [VMEM] * 2, [((SEGLEN, DETS), f32), ((PLANE, 8, SEGL...  2.39 us
    ppermute x1, waiting for transfers between devices, local(): beyond = lax.ppermute(message, ('z', 'yh'), swap_pairs())  2.05 us
  transfers between devices with their start and end apart: 2, of which 2 were waited for; matrix products, arithmetic and copies ran while one was open for 0% of the time, Pallas kernels for 1%

profile of v2, /device:TPU:1, one launch (start us, length us, event | category | flops | bytes accessed | tf_op | source)
XLA Modules:
  0.0 85.2 jit_solution(12959764386482653967)
XLA Ops:
  0.0 0.0 copy-start
  0.0 4.0 %weight.1 = f32[1024,128]{1,0:T(8,128)} custom-call(f32[4]{0:T(128)} %knee_hbm.1, f32[4]{0:T(128)} %slope_hbm.1, f32[4]{0:T(128)} %level_hbm.1, f32[1024,128]{1,0:T(8,128)} %bitcast.17, bf16[4,256,256]{2,1,0:T(8,128)(2,1)} %constant.34.clone.tables_hbm, f32[3,136,128]{2,1,0:T(8,128)} %constant.35.clone.factors_hbm), custom_call_target="tpu_custom_call" | custom-call | tf_op jit(solution)/shard_map/weight/pallas_call | solution.py:264
  4.0 0.0 copy-start.3
  4.0 0.0 copy-start.1
  4.0 0.0 copy-start.2
  4.0 35.6 %all_to_all.20 = f32[256,4,128]{2,1,0:T(4,128)S(1)} all-to-all(f32[256,4,128]{2,1,0:T(4,128)} %bitcast.16), channel_id=1, replica_groups=mesh['z'=8,'yh'=2,'yl'=2,'x'=4,'c'=2] {'z','yh','yl','x','c'}, dimensions={0} | all-to-all | bytes 1048576 | tf_op jit(solution)/shard_map/all_to_all | solution.py:267
  39.6 0.0 copy-done
  39.6 2.4 %project.1 = (f32[128,1024]{1,0:T(8,128)S(1)}, f32[32,8,128]{2,1,0:T(8,128)}) custom-call(f32[1024,128]{1,0:T(8,128)S(1)} %bitcast.13, f32[1024,512]{1,0:T(8,128)S(1)} %copy-done), custom_call_target="tpu_custom_call" | custom-call | tf_op jit(solution)/shard_map/project/pallas_call | solution.py:273
  42.0 5.0 %all-to-all-start.1 = ((f32[32,8,128]{2,1,0:T(8,128)}), f32[32,8,128]{2,1,0:T(8,128)S(1)}, u32[]{:S(2)}, u32[]{:S(2)}) async-start(f32[32,8,128]{2,1,0:T(8,128)} %get-tuple-element.11), calls=%async_computation.1 | async-start | bytes 262144 | tf_op jit(solution)/shard_map/all_to_all | solution.py:276
  47.0 7.6 %all-to-all-done.1.gathered_ref = f32[32,8,128]{2,1,0:T(8,128)S(1)} async-done(((f32[32,8,128]{2,1,0:T(8,128)}), f32[32,8,128]{2,1,0:T(8,128)S(1)}, u32[]{:S(2)}, u32[]{:S(2)}) %all-to-all-start.1) | async-done | bytes 131104 | tf_op jit(solution)/shard_map/all_to_all | solution.py:276
  54.6 0.0 copy-done.3
  54.6 0.9 %halo.1 = (f32[8,128]{1,0:T(8,128)S(1)}, f32[8,128]{1,0:T(8,128)S(1)}, f32[8,128]{1,0:T(8,128)S(1)}) custom-call(s32[33]{0:T(128)S(1)} %copy-done.3, s32[1]{0:T(128)} %bitcast.5.segment_ref, f32[32,8,128]{2,1,0:T(8,128)S(1)} %all-to-all-done.1.gathered_ref), custom_call_target="tpu_custom_call" | custom-call | tf_op jit(solution)/shard_map/halo/pallas_call | solution.py:277
  55.5 1.2 %collective-permute-start = (f32[8,128]{1,0:T(8,128)S(1)}, f32[8,128]{1,0:T(8,128)S(1)}, u32[]{:S(2)}, u32[]{:S(2)}) collective-permute-start(f32[8,128]{1,0:T(8,128)S(1)} %get-tuple-element.14), channel_id=1, source_target_pairs={{0,224},{16,48},{32,64},{48,16},{64,32},{80,112},{96,128},{112,80}... | collective-permute-start | bytes 12296 | tf_op jit(solution)/shard_map/ppermute | solution.py:280
  56.7 0.0 copy-done.1
  56.7 0.0 copy-done.2
  56.7 0.5 slots.1.hot_ref
  57.2 2.0 %collective-permute-done.message_ref = f32[8,128]{1,0:T(8,128)S(1)} collective-permute-done((f32[8,128]{1,0:T(8,128)S(1)}, f32[8,128]{1,0:T(8,128)S(1)}, u32[]{:S(2)}, u32[]{:S(2)}) %collective-permute-start) | collective-permute-done | bytes 4128 | tf_op jit(solution)/shard_map/ppermute | solution.py:280
  59.2 0.4 bin.1
  59.7 11.9 %all_to_all.21.parts_ref = f32[32,8,128]{2,1,0:T(8,128)S(1)} all-to-all(f32[32,8,128]{2,1,0:T(8,128)S(1)} %bitcast.14), channel_id=1, replica_groups=mesh['z'=8,'yh'=2,'yl'=2,'x'=4,'c'=2] {'yh','yl','x','c'}, dimensions={0} | all-to-all | bytes 262144 | tf_op jit(solution)/shard_map/all_to_all | solution.py:282
  71.7 12.9 %all_to_all.22 = f32[32,8,128]{2,1,0:T(8,128)S(1)} all-to-all(f32[32,8,128]{2,1,0:T(8,128)S(1)} %fold.1), channel_id=1, replica_groups=mesh['z'=8,'yh'=2,'yl'=2,'x'=4,'c'=2] {'z','yh','yl'}, dimensions={0} | all-to-all | bytes 262144 | tf_op jit(solution)/shard_map/all_to_all | solution.py:286
  84.6 0.6 bitcast_reduce_fusion
  (1 shorter events, 0.0 us)
Async XLA Ops:
  0.0 39.6 %copy-start = (f32[1024,512]{1,0:T(8,128)S(1)}, f32[1024,512]{1,0:T(8,128)}, u32[]{:S(2)}) copy-start(f32[1024,512]{1,0:T(8,128)} %templates_ref.1) | copy-start | bytes 6291460
  4.0 50.6 %copy-start.3 = (s32[33]{0:T(128)S(1)}, s32[33]{0:T(128)}, u32[]{:S(2)}) copy-start(s32[33]{0:T(128)} %bounds_ref.1) | copy-start | bytes 400
  4.0 52.7 %copy-start.1 = (s32[1024,256]{1,0:T(8,128)S(1)}, s32[1024,256]{1,0:T(8,128)}, u32[]{:S(2)}) copy-start(s32[1024,256]{1,0:T(8,128)} %index_ref.1) | copy-start | bytes 3145732
  4.0 52.7 %copy-start.2 = (s32[256]{0:T(256)S(1)}, s32[256]{0:T(256)}, u32[]{:S(2)}) copy-start(s32[256]{0:T(256)} %param.17) | copy-start | bytes 3076
  42.0 12.6 %all-to-all-start.1 = ((f32[32,8,128]{2,1,0:T(8,128)}), f32[32,8,128]{2,1,0:T(8,128)S(1)}, u32[]{:S(2)}, u32[]{:S(2)}) async-start(f32[32,8,128]{2,1,0:T(8,128)} %get-tuple-element.11), calls=%async_computation.1 | async-start | bytes 262144 | tf_op jit(solution)/shard_map/all_to_all | solution.py:276
  55.5 3.8 %collective-permute-start = (f32[8,128]{1,0:T(8,128)S(1)}, f32[8,128]{1,0:T(8,128)S(1)}, u32[]{:S(2)}, u32[]{:S(2)}) collective-permute-start(f32[8,128]{1,0:T(8,128)S(1)} %get-tuple-element.14), channel_id=1, source_target_pairs={{0,224},{16,48},{32,64},{48,16},{64,32},{80,112},{96,128},{112,80}... | collective-permute-start | bytes 12296 | tf_op jit(solution)/shard_map/ppermute | solution.py:280

commit v3 on v2

--- a/solution.py
+++ b/solution.py
@@ -20,10 +20,10 @@
 HALF = SEGMENTS // 2
 ROWS = HALF + 8
 GROUP = 16
-GROUPS = SEGMENTS // GROUP
 PLANE = 2 * GROUP
 MAP_SCALE = 1.0 / math.sqrt(DETS * SAMPLES // (SEGLEN * BLOCKS))
-ALL = ("z", "yh", "yl", "x", "c")
+ALL = ("z", "y", "x", "c")
+PLANES = 8
 bf16 = jnp.bfloat16
 f32 = jnp.float32
 
@@ -71,19 +71,19 @@
 TN = ((0,), (0,))
 
 
-def group_at(block):
-    z, yh = divmod(block, 2)
-    return 2 * z + (yh ^ (z & 1))
+def held_at(plane, core):
+    return PLANE * ((plane + core) % PLANES) + GROUP * (1 - core)
 
 
 def weight_kernel(
-    knee_hbm, slope_hbm, level_hbm, x_hbm, tables_hbm, factors_hbm, out_ref,
-    knee_ref, slope_ref, level_ref, x_ref, tables_ref, factors_ref, sems,
+    knee_hbm, slope_hbm, level_hbm, x_hbm, tables_hbm, factors_hbm, out_hbm,
+    knee_ref, slope_ref, level_ref, x_ref, outer_ref, inner_ref, factors_ref, out_ref, sems, out_sems,
 ):
     pairs = [
         (x_hbm, x_ref),
-        (tables_hbm, tables_ref),
+        (tables_hbm.at[pl.ds(0, 2)], outer_ref),
         (factors_hbm, factors_ref),
+        (tables_hbm.at[pl.ds(2, 2)], inner_ref),
         (knee_hbm, knee_ref),
         (slope_hbm, slope_ref),
         (level_hbm, level_ref),
@@ -91,14 +91,16 @@
     copies = [pltpu.make_async_copy(src, dst, sems.at[i]) for i, (src, dst) in enumerate(pairs)]
     for copy in copies:
         copy.start()
-    for copy in copies:
-        copy.wait()
+    copies[0].wait()
+    copies[1].wait()
     parts = [split(x_ref[pl.ds(d, SEGMENTS, stride=OWN_DETS), :]) for d in range(OWN_DETS)]
-    outer = (tables_ref[0], tables_ref[1])
-    inner = (tables_ref[2], tables_ref[3])
-    cos, sin, log_fold = factors_ref[0], factors_ref[1], factors_ref[2]
+    outer = (outer_ref[0], outer_ref[1])
     samples = tuple(jnp.concatenate([part[i] for part in parts], axis=1) for i in range(2))
     section = dot3(outer, samples, NN)
+    for copy in copies[2:]:
+        copy.wait()
+    inner = (inner_ref[0], inner_ref[1])
+    cos, sin, log_fold = factors_ref[0], factors_ref[1], factors_ref[2]
     top = lax.broadcasted_iota(jnp.int32, (8, SEGLEN), 0) == 0
     stacked = []
     for d in range(OWN_DETS):
@@ -130,28 +132,20 @@
         first = jnp.where(top, jnp.broadcast_to(turn_re[HALF : HALF + 1], (8, SEGLEN)), turn_im[:8])
         turned.append(jnp.concatenate([turn_re[:HALF], first, turn_im[8:HALF]], axis=0))
     result = dot3(outer, split(jnp.concatenate(turned, axis=1)), TN)
-    for d in range(OWN_DETS):
-        for block in range(GROUPS):
-            start = GROUP * group_at(block)
-            out_ref[pl.ds(GROUP * OWN_DETS * block + d, GROUP, stride=OWN_DETS), :] = result[
-                start : start + GROUP, SEGLEN * d : SEGLEN * (d + 1)
-            ]
-
-
-def slot_kernel(segment_ref, index_ref, slot_ref, hot_ref):
-    pick = lax.broadcasted_iota(jnp.int32, (8, SEGMENTS), 1) == segment_ref[0]
-    index = index_ref[...].astype(f32).astype(bf16)
-    seen = lax.dot_general(
-        jnp.where(pick, 1.0, 0.0).astype(bf16), index, (NT, ((), ())), preferred_element_type=f32
-    )
-    block = lax.broadcasted_iota(jnp.int32, (BLOCKS, DETS), 0)
-    hot = jnp.where(jnp.broadcast_to(seen[0:1].astype(jnp.int32), (BLOCKS, DETS)) == block, 1.0, 0.0).astype(bf16)
-    table = jnp.broadcast_to(slot_ref[...].astype(f32).astype(bf16), (8, BLOCKS))
-    slot = lax.dot_general(table, hot, (NN, ((), ())), preferred_element_type=f32)
-    row = ((block >> 3) & 7) * 32 + (block >> 6) * 8 + (block & 7)
-    hot_ref[...] = jnp.where(
-        jnp.broadcast_to(slot[0:1].astype(jnp.int32), (BLOCKS, DETS)) == row, 1.0, 0.0
-    ).astype(bf16)
+    writes = []
+    for plane in range(PLANES):
+        for core in range(2):
+            start = held_at(plane, core)
+            for d in range(OWN_DETS):
+                row = (PLANE * plane + core) * OWN_DETS + d
+                out_ref[pl.ds(row, GROUP, stride=2 * OWN_DETS), :] = result[
+                    start : start + GROUP, SEGLEN * d : SEGLEN * (d + 1)
+                ]
+        rows = pl.ds(PLANE * OWN_DETS * plane, PLANE * OWN_DETS)
+        writes.append(pltpu.make_async_copy(out_ref.at[rows], out_hbm.at[rows], out_sems.at[plane]))
+        writes[-1].start()
+    for write in writes:
+        write.wait()
 
 
 def project_kernel(data_ref, templates_ref, clean_ref, power_ref):
@@ -177,29 +171,46 @@
     return first // SEGLEN, end // SEGLEN
 
 
-def masked_sum(gathered_ref, base, turn, first, end):
-    total = jnp.zeros((8, SEGLEN), f32)
-    for member in range(PLANE):
-        at = base + (member ^ turn)
-        inside = (at >= first) & (at < end)
-        total = total + jnp.where(inside, 1.0, 0.0) * gathered_ref[member]
-    return total
-
-
-def halo_kernel(bounds_ref, segment_ref, gathered_ref, own_ref, share_ref, message_ref):
+def prepare_kernel(
+    segment_ref, bounds_ref, index_ref, slot_ref, hot_ref, weight_ref, beyond_ref, share_ref
+):
     segment = segment_ref[0]
-    plane = segment // PLANE
-    base = plane * PLANE
-    turn = (plane & 1) * GROUP
+    base = segment // PLANE * PLANE
     late = (segment & GROUP) != 0
     first, end = interval_of(bounds_ref, segment)
-    length = jnp.full((8, SEGLEN), (end - first) * SEGLEN, jnp.int32).astype(f32)
-    own_ref[...] = masked_sum(gathered_ref, base, turn, first, end) / length + EPS
-    beyond = jnp.where(late, end > base + PLANE, first < base)
-    share_ref[...] = jnp.where(beyond, 1.0, 0.0) / length
-    first, end = interval_of(bounds_ref, jnp.where(late, base + PLANE, base - 1))
+    part = 1.0 / jnp.full((8, SEGLEN), (end - first) * SEGLEN, jnp.int32).astype(f32)
+    share_ref[...] = jnp.where(jnp.where(late, end > base + PLANE, first < base), part, 0.0)
+    next_first, next_end = interval_of(bounds_ref, jnp.where(late, base + PLANE, base - 1))
     edge = jnp.where(late, base + PLANE == SEGMENTS, base == 0)
-    message_ref[...] = masked_sum(gathered_ref, base, turn, jnp.where(edge, end, first), end)
+    next_first = jnp.where(edge, next_end, next_first)
+    for member in range(PLANE):
+        at = base + member
+        weight_ref[member] = jnp.where((at >= first) & (at < end), part, 0.0)
+        beyond_ref[member] = jnp.full((8, SEGLEN), jnp.where((at >= next_first) & (at < next_end), 1.0, 0.0), f32)
+    pick = lax.broadcasted_iota(jnp.int32, (8, SEGMENTS), 1) == segment
+    index = index_ref[...].astype(f32).astype(bf16)
+    seen = lax.dot_general(
+        jnp.where(pick, 1.0, 0.0).astype(bf16), index, (NT, ((), ())), preferred_element_type=f32
+    )
+    block = lax.broadcasted_iota(jnp.int32, (BLOCKS, DETS), 0)
+    hot = jnp.where(jnp.broadcast_to(seen[0:1].astype(jnp.int32), (BLOCKS, DETS)) == block, 1.0, 0.0).astype(bf16)
+    table = jnp.broadcast_to(slot_ref[...].astype(f32).astype(bf16), (8, BLOCKS))
+    slot = lax.dot_general(table, hot, (NN, ((), ())), preferred_element_type=f32)
+    row = ((block >> 3) & 7) * 32 + (block >> 6) * 8 + (block & 7)
+    hot_ref[...] = jnp.where(
+        jnp.broadcast_to(slot[0:1].astype(jnp.int32), (BLOCKS, DETS)) == row, 1.0, 0.0
+    ).astype(bf16)
+
+
+def halo_kernel(gathered_ref, weight_ref, beyond_ref, own_ref, message_ref):
+    own = jnp.full((8, SEGLEN), EPS, f32)
+    message = jnp.zeros((8, SEGLEN), f32)
+    for member in range(PLANE):
+        power = gathered_ref[member]
+        own = own + weight_ref[member] * power
+        message = message + beyond_ref[member] * power
+    own_ref[...] = own
+    message_ref[...] = message
 
 
 def bin_kernel(clean_ref, own_ref, share_ref, message_ref, hot_ref, map_ref):
@@ -228,67 +239,68 @@
 HBM = pl.BlockSpec(memory_space=pltpu.HBM)
 
 
-def call(kernel, specs, outs, name, scratch=(), mib=16):
+def call(kernel, specs, outs, name, scratch=(), mib=16, out_spec=VMEM):
     shapes = [jax.ShapeDtypeStruct(shape, dtype) for shape, dtype in outs]
     return pl.pallas_call(
         kernel,
         out_shape=shapes if len(shapes) > 1 else shapes[0],
         in_specs=specs,
-        out_specs=[VMEM] * len(shapes) if len(shapes) > 1 else VMEM,
+        out_specs=[out_spec] * len(shapes) if len(shapes) > 1 else out_spec,
         scratch_shapes=list(scratch),
         compiler_params=pltpu.CompilerParams(vmem_limit_bytes=mib * 1024 * 1024),
         name=name,
     )
 
 
-def swap_pairs():
-    pairs = []
-    for z in range(8):
-        for yh in range(2):
-            z_to = z ^ 1 if yh else (z + (1 if z % 2 else -1)) % 8
-            pairs.append((2 * z + yh, 2 * z_to + yh))
-    return pairs
+def interval_groups():
+    groups = []
+    for k in range(PLANES):
+        early = [PLANE * ((k - 1) % PLANES) + 2 * m + 1 for m in range(GROUP)]
+        groups.append(early + [PLANE * k + 2 * m for m in range(GROUP)])
+    return groups
 
 
 def local(timelines, knee_freq, noise_slope, noise_level, templates, interval_bounds, block_index, block_slot):
-    z, yh = lax.axis_index("z"), lax.axis_index("yh")
-    member = lax.axis_index(("yl", "x", "c"))
-    segment = ((2 * z + (yh ^ (z & 1))) * GROUP + member).astype(jnp.int32).reshape(1)
+    core = lax.axis_index("c")
+    group = lax.rem(lax.axis_index("z") + core, PLANES)
+    segment = (PLANE * group + GROUP * (1 - core) + lax.axis_index(("y", "x"))).astype(jnp.int32).reshape(1)
     rows = timelines.reshape(OWN_DETS, SEGMENTS, SEGLEN).transpose(1, 0, 2).reshape(DETS, SEGLEN)
     scratch = [pltpu.SMEM((OWN_DETS,), f32)] * 3 + [
         pltpu.VMEM((DETS, SEGLEN), f32),
-        pltpu.VMEM((4, SEGMENTS, SEGMENTS), bf16),
+        pltpu.VMEM((2, SEGMENTS, SEGMENTS), bf16),
+        pltpu.VMEM((2, SEGMENTS, SEGMENTS), bf16),
         pltpu.VMEM((3, ROWS, SEGLEN), f32),
-        pltpu.SemaphoreType.DMA((6,)),
+        pltpu.VMEM((DETS, SEGLEN), f32),
+        pltpu.SemaphoreType.DMA((7,)),
+        pltpu.SemaphoreType.DMA((PLANES,)),
     ]
-    weighted = call(weight_kernel, [HBM] * 6, [((DETS, SEGLEN), f32)], "weight", scratch, 60)(
+    weighted = call(weight_kernel, [HBM] * 6, [((DETS, SEGLEN), f32)], "weight", scratch, 60, HBM)(
         knee_freq, noise_slope, noise_level, rows, *[jnp.asarray(t) for t in tables()]
     )
     data = lax.all_to_all(
         weighted.reshape(SEGMENTS, OWN_DETS, SEGLEN), ALL, split_axis=0, concat_axis=0, tiled=True
     ).reshape(DETS, SEGLEN)
-    hot = call(slot_kernel, [SMEM] + [VMEM] * 2, [((BLOCKS, DETS), bf16)], "slots")(
-        segment, block_index, block_slot.reshape(1, BLOCKS)
-    )
-    cleaned, power = call(
-        project_kernel, [VMEM] * 2, [((SEGLEN, DETS), f32), ((PLANE, 8, SEGLEN), f32)], "project"
-    )(data, templates)
-    gathered = lax.all_to_all(power, ("yh", "yl", "x", "c"), split_axis=0, concat_axis=0, tiled=True)
-    own, share, message = call(halo_kernel, [SMEM] * 2 + [VMEM], [((8, SEGLEN), f32)] * 3, "halo")(
-        interval_bounds, segment, gathered
-    )
-    beyond = lax.ppermute(message, ("z", "yh"), swap_pairs())
+    line, lines = ((8, SEGLEN), f32), ((PLANE, 8, SEGLEN), f32)
+    cleaned, power = call(project_kernel, [VMEM] * 2, [((SEGLEN, DETS), f32), lines], "project")(data, templates)
+    gathered = lax.all_to_all(
+        power, ALL, split_axis=0, concat_axis=0, axis_index_groups=interval_groups(), tiled=True
+    )
+    hot, inside, outside, share = call(
+        prepare_kernel, [SMEM] * 2 + [VMEM] * 2, [((BLOCKS, DETS), bf16), lines, lines, line], "prepare"
+    )(segment, interval_bounds, block_index, block_slot.reshape(1, BLOCKS))
+    own, message = call(halo_kernel, [VMEM] * 3, [line] * 2, "halo")(gathered, inside, outside)
+    beyond = lax.ppermute(message, "c", [(0, 1), (1, 0)])
     partial = call(bin_kernel, [VMEM] * 5, [((BLOCKS, SEGLEN), f32)], "bin")(cleaned, own, share, beyond, hot)
     spread = lax.all_to_all(
-        partial.reshape(32, 8, SEGLEN), ("yh", "yl", "x", "c"), split_axis=0, concat_axis=0, tiled=True
+        partial.reshape(32, 8, SEGLEN), ("y", "x", "c"), split_axis=0, concat_axis=0, tiled=True
     )
     copies = call(fold_kernel, [VMEM], [((32, 8, SEGLEN), f32)], "fold")(spread)
-    sums = lax.all_to_all(copies, ("z", "yh", "yl"), split_axis=0, concat_axis=0, tiled=True)
+    sums = lax.all_to_all(copies, ("z", "y"), split_axis=0, concat_axis=0, tiled=True)
     return jnp.sum(sums.reshape(8, 32, SEGLEN), axis=0)
 
 
 def solution(mesh):
-    whole = Mesh(mesh.devices.reshape(8, 2, 2, 4, 2), ALL)
+    whole = Mesh(mesh.devices.reshape(8, 4, 4, 2), ALL)
     return jax.shard_map(
         local,
         mesh=whole,

time: 85.5 us -> 83.7 us (0.979)
  waiting for transfers between devices: 9.66 us -> 8.01 us
    ppermute x1, waiting for transfers between devices: 2.05 us -> 0.82 us  [local(): beyond = lax.ppermute(message, 'c', [(0, 1), (1, 0)])]
where the time goes in v3:
time: 83.7 us; the launch traced here: 83.4 us
  blocking collectives  60.4 us (72%)
  waiting for transfers between devices  8.01 us (10%)
  Pallas kernels  7.82 us (9%)
  starting transfers between devices  6.48 us (8%)
    all_to_all x1, blocking collectives, local(): lax.all_to_all(weighted.reshape(SEGMENTS, OWN_DETS, SEGLEN), ALL, split_a...  35.6 us
    all_to_all x1, blocking collectives, local(): lax.all_to_all(copies, ('z', 'y'), split_axis=0, concat_axis=0, tiled=True)  13.8 us
    all_to_all x1, blocking collectives, local(): lax.all_to_all(partial.reshape(32, 8, SEGLEN), ('y', 'x', 'c'), split_axi...  11 us
    all_to_all x1, waiting for transfers between devices, local(): lax.all_to_all(power, ALL, split_axis=0, concat_axis=0, axis_index_groups...  7.18 us
    all_to_all x1, starting transfers between devices, local(): lax.all_to_all(power, ALL, split_axis=0, concat_axis=0, axis_index_groups...  5.31 us
    pallas_call x1, Pallas kernels, local(): call(weight_kernel, [HBM] * 6, [((DETS, SEGLEN), f32)], 'weight', scratch...  3.88 us
    pallas_call x1, Pallas kernels, local(): call(project_kernel, [VMEM] * 2, [((SEGLEN, DETS), f32), lines], 'project')  2.4 us
  transfers between devices with their start and end apart: 2, of which 2 were waited for; matrix products, arithmetic and copies ran while one was open for 0% of the time, Pallas kernels for 1%

profile of v3, /device:TPU:1, one launch (start us, length us, event | category | flops | bytes accessed | tf_op | source)
XLA Modules:
  0.0 83.4 jit_solution(8559143449372612199)
XLA Ops:
  0.0 0.0 copy-start
  0.0 3.9 %weight.1 = f32[1024,128]{1,0:T(8,128)} custom-call(f32[4]{0:T(128)} %knee_hbm.1, f32[4]{0:T(128)} %slope_hbm.1, f32[4]{0:T(128)} %level_hbm.1, f32[1024,128]{1,0:T(8,128)} %bitcast.17, bf16[4,256,256]{2,1,0:T(8,128)(2,1)} %constant.35.clone.tables_hbm, f32[3,136,128]{2,1,0:T(8,128)} %constant.36.clone.factors_hbm), custom_call_target="tpu_custom_call" | custom-call | tf_op jit(solution)/shard_map/weight/pallas_call | solution.py:277
  3.9 0.0 copy-start.1
  3.9 0.0 copy-start.2
  3.9 0.0 copy-start.3
  3.9 35.6 %all_to_all.20 = f32[256,4,128]{2,1,0:T(4,128)S(1)} all-to-all(f32[256,4,128]{2,1,0:T(4,128)} %bitcast.16), channel_id=1, replica_groups=mesh['z'=8,'y'=4,'x'=4,'c'=2] {'z','y','x','c'}, dimensions={0} | all-to-all | bytes 1048576 | tf_op jit(solution)/shard_map/all_to_all | solution.py:280
  39.5 0.0 copy-done
  39.5 2.4 %project.1 = (f32[128,1024]{1,0:T(8,128)S(1)}, f32[32,8,128]{2,1,0:T(8,128)}) custom-call(f32[1024,128]{1,0:T(8,128)S(1)} %bitcast.13, f32[1024,512]{1,0:T(8,128)S(1)} %copy-done), custom_call_target="tpu_custom_call" | custom-call | tf_op jit(solution)/shard_map/project/pallas_call | solution.py:284
  41.9 5.3 %all-to-all-start.1 = ((f32[32,8,128]{2,1,0:T(8,128)}), f32[32,8,128]{2,1,0:T(8,128)S(1)}, u32[]{:S(2)}, u32[]{:S(2)}) async-start(f32[32,8,128]{2,1,0:T(8,128)} %get-tuple-element.14), calls=%async_computation.1 | async-start | bytes 262144 | tf_op jit(solution)/shard_map/all_to_all | solution.py:285
  47.2 0.0 copy-done.1
  47.2 0.0 copy-done.2
  47.2 0.0 copy-done.3
  47.2 1.0 %prepare.1 = (bf16[256,1024]{1,0:T(8,128)(2,1)S(1)}, f32[32,8,128]{2,1,0:T(8,128)S(1)}, f32[32,8,128]{2,1,0:T(8,128)S(1)}, f32[8,128]{1,0:T(8,128)S(1)}) custom-call(s32[1]{0:T(128)} %bitcast.5.segment_ref, s32[33]{0:T(128)S(1)} %copy-done.3, s32[1024,256]{1,0:T(8,128)S(1)} %copy-done.1, s32[1,256]{1,0:T(1,128)S(1)} %bitcast.15), custom_call_target="tpu_custom_call" | custom-call | tf_op jit(solution)/shard_map/prepare/pallas_call | solution.py:288
  48.3 7.2 %all-to-all-done.1.gathered_ref = f32[32,8,128]{2,1,0:T(8,128)S(1)} async-done(((f32[32,8,128]{2,1,0:T(8,128)}), f32[32,8,128]{2,1,0:T(8,128)S(1)}, u32[]{:S(2)}, u32[]{:S(2)}) %all-to-all-start.1) | async-done | bytes 131104 | tf_op jit(solution)/shard_map/all_to_all | solution.py:285
  55.5 1.2 %collective-permute-start = (f32[8,128]{1,0:T(8,128)S(1)}, f32[8,128]{1,0:T(8,128)S(1)}, u32[]{:S(2)}, u32[]{:S(2)}) collective-permute-start(f32[8,128]{1,0:T(8,128)S(1)} %get-tuple-element.19), channel_id=1, source_target_pairs={{0,1},{1,0},{2,3},{3,2},{4,5},{5,4},{6,7},{7,6},{8,9},{9,8},{10,11... | collective-permute-start | bytes 12296 | tf_op jit(solution)/shard_map/ppermute | solution.py:292
  56.7 0.8 collective-permute-done.message_ref
  57.5 0.4 bin.1
  57.9 11.0 %all_to_all.21.parts_ref = f32[32,8,128]{2,1,0:T(8,128)S(1)} all-to-all(f32[32,8,128]{2,1,0:T(8,128)S(1)} %bitcast.14), channel_id=1, replica_groups=mesh['z'=8,'y'=4,'x'=4,'c'=2] {'y','x','c'}, dimensions={0} | all-to-all | bytes 262144 | tf_op jit(solution)/shard_map/all_to_all | solution.py:294
  69.0 13.8 %all_to_all.22 = f32[32,8,128]{2,1,0:T(8,128)S(1)} all-to-all(f32[32,8,128]{2,1,0:T(8,128)S(1)} %fold.1), channel_id=1, replica_groups=mesh['z'=8,'y'=4,'x'=4,'c'=2] {'z','y'}, dimensions={0} | all-to-all | bytes 262144 | tf_op jit(solution)/shard_map/all_to_all | solution.py:298
  82.8 0.6 bitcast_reduce_fusion
  (2 shorter events, 0.1 us)
Async XLA Ops:
  0.0 39.5 %copy-start = (f32[1024,512]{1,0:T(8,128)S(1)}, f32[1024,512]{1,0:T(8,128)}, u32[]{:S(2)}) copy-start(f32[1024,512]{1,0:T(8,128)} %templates_ref.1) | copy-start | bytes 6291460
  3.9 43.3 %copy-start.1 = (s32[1024,256]{1,0:T(8,128)S(1)}, s32[1024,256]{1,0:T(8,128)}, u32[]{:S(2)}) copy-start(s32[1024,256]{1,0:T(8,128)} %index_ref.1) | copy-start | bytes 3145732
  3.9 43.3 %copy-start.2 = (s32[256]{0:T(256)S(1)}, s32[256]{0:T(256)}, u32[]{:S(2)}) copy-start(s32[256]{0:T(256)} %param.17) | copy-start | bytes 3076
  3.9 43.3 %copy-start.3 = (s32[33]{0:T(128)S(1)}, s32[33]{0:T(128)}, u32[]{:S(2)}) copy-start(s32[33]{0:T(128)} %bounds_ref.1) | copy-start | bytes 400
  41.9 13.6 %all-to-all-start.1 = ((f32[32,8,128]{2,1,0:T(8,128)}), f32[32,8,128]{2,1,0:T(8,128)S(1)}, u32[]{:S(2)}, u32[]{:S(2)}) async-start(f32[32,8,128]{2,1,0:T(8,128)} %get-tuple-element.14), calls=%async_computation.1 | async-start | bytes 262144 | tf_op jit(solution)/shard_map/all_to_all | solution.py:285
  55.5 2.0 %collective-permute-start = (f32[8,128]{1,0:T(8,128)S(1)}, f32[8,128]{1,0:T(8,128)S(1)}, u32[]{:S(2)}, u32[]{:S(2)}) collective-permute-start(f32[8,128]{1,0:T(8,128)S(1)} %get-tuple-element.19), channel_id=1, source_target_pairs={{0,1},{1,0},{2,3},{3,2},{4,5},{5,4},{6,7},{7,6},{8,9},{9,8},{10,11... | collective-permute-start | bytes 12296 | tf_op jit(solution)/shard_map/ppermute | solution.py:292

commit v4 on v3

--- a/solution.py
+++ b/solution.py
@@ -49,7 +49,7 @@
     fold = np.minimum(freq, SAMPLES - freq)
     log_fold = np.where(fold > 0, np.log(np.maximum(fold, 1)), 0.0)
     return (
-        np.stack([*split_np(outer), *split_np(inner)]),
+        np.stack([*split_np(outer), *split_np(inner), *split_np(outer.T)]),
         np.stack([np.cos(angle), np.sin(angle), log_fold]).astype(np.float32),
     )
 
@@ -63,23 +63,54 @@
     def one(x, y):
         return lax.dot_general(x, y, (dims, ((), ())), preferred_element_type=f32)
 
-    return one(a[0], b[0]) + (one(a[0], b[1]) + one(a[1], b[0]))
+    rows = a[0].shape[0]
+    both = one(jnp.concatenate(a, axis=0), b[0])
+    return both[:rows] + (both[rows:] + one(a[0], b[1]))
 
 
 NN = ((1,), (0,))
 NT = ((1,), (1,))
-TN = ((0,), (0,))
 
 
 def held_at(plane, core):
     return PLANE * ((plane + core) % PLANES) + GROUP * (1 - core)
 
 
+def interval_of(bounds_ref, segment):
+    at = segment * SEGLEN
+    first = jnp.int32(0)
+    end = jnp.int32(SAMPLES)
+    for t in range(1, INTERVALS):
+        bound = bounds_ref[t]
+        first = jnp.where(bound <= at, jnp.maximum(first, bound), first)
+        end = jnp.where(bound > at, jnp.minimum(end, bound), end)
+    return first // SEGLEN, end // SEGLEN
+
+
+def member_weights(bounds_ref, inside_ref, outside_ref, share_ref):
+    core = lax.axis_index("c")
+    base = PLANE * lax.rem(lax.axis_index("z") + core, PLANES)
+    segment = base + GROUP * (1 - core) + 4 * lax.axis_index("y") + lax.axis_index("x")
+    late = core == 0
+    first, end = interval_of(bounds_ref, segment)
+    part = 1.0 / jnp.full((8, SEGLEN), (end - first) * SEGLEN, jnp.int32).astype(f32)
+    share_ref[...] = jnp.where(jnp.where(late, end > base + PLANE, first < base), part, 0.0)
+    next_first, next_end = interval_of(bounds_ref, jnp.where(late, base + PLANE, base - 1))
+    edge = jnp.where(late, base + PLANE == SEGMENTS, base == 0)
+    next_first = jnp.where(edge, next_end, next_first)
+    for member in range(PLANE):
+        at = base + member
+        inside_ref[member] = jnp.where((at >= first) & (at < end), part, 0.0)
+        outside_ref[member] = jnp.full((8, SEGLEN), jnp.where((at >= next_first) & (at < next_end), 1.0, 0.0), f32)
+
+
 def weight_kernel(
-    knee_hbm, slope_hbm, level_hbm, x_hbm, tables_hbm, factors_hbm, out_hbm,
-    knee_ref, slope_ref, level_ref, x_ref, outer_ref, inner_ref, factors_ref, out_ref, sems, out_sems,
+    bounds_hbm, knee_hbm, slope_hbm, level_hbm, x_hbm, tables_hbm, factors_hbm,
+    out_ref, inside_ref, outside_ref, share_ref,
+    bounds_ref, knee_ref, slope_ref, level_ref, x_ref, outer_ref, inner_ref, back_ref, factors_ref, sems,
 ):
     pairs = [
+        (bounds_hbm, bounds_ref),
         (x_hbm, x_ref),
         (tables_hbm.at[pl.ds(0, 2)], outer_ref),
         (factors_hbm, factors_ref),
@@ -87,17 +118,20 @@
         (knee_hbm, knee_ref),
         (slope_hbm, slope_ref),
         (level_hbm, level_ref),
+        (tables_hbm.at[pl.ds(4, 2)], back_ref),
     ]
     copies = [pltpu.make_async_copy(src, dst, sems.at[i]) for i, (src, dst) in enumerate(pairs)]
     for copy in copies:
         copy.start()
     copies[0].wait()
+    member_weights(bounds_ref, inside_ref, outside_ref, share_ref)
     copies[1].wait()
+    copies[2].wait()
     parts = [split(x_ref[pl.ds(d, SEGMENTS, stride=OWN_DETS), :]) for d in range(OWN_DETS)]
     outer = (outer_ref[0], outer_ref[1])
     samples = tuple(jnp.concatenate([part[i] for part in parts], axis=1) for i in range(2))
     section = dot3(outer, samples, NN)
-    for copy in copies[2:]:
+    for copy in copies[3:8]:
         copy.wait()
     inner = (inner_ref[0], inner_ref[1])
     cos, sin, log_fold = factors_ref[0], factors_ref[1], factors_ref[2]
@@ -131,8 +165,8 @@
         turn_im = imag * cos + real * sin
         first = jnp.where(top, jnp.broadcast_to(turn_re[HALF : HALF + 1], (8, SEGLEN)), turn_im[:8])
         turned.append(jnp.concatenate([turn_re[:HALF], first, turn_im[8:HALF]], axis=0))
-    result = dot3(outer, split(jnp.concatenate(turned, axis=1)), TN)
-    writes = []
+    copies[8].wait()
+    result = dot3((back_ref[0], back_ref[1]), split(jnp.concatenate(turned, axis=1)), NN)
     for plane in range(PLANES):
         for core in range(2):
             start = held_at(plane, core)
@@ -141,11 +175,6 @@
                 out_ref[pl.ds(row, GROUP, stride=2 * OWN_DETS), :] = result[
                     start : start + GROUP, SEGLEN * d : SEGLEN * (d + 1)
                 ]
-        rows = pl.ds(PLANE * OWN_DETS * plane, PLANE * OWN_DETS)
-        writes.append(pltpu.make_async_copy(out_ref.at[rows], out_hbm.at[rows], out_sems.at[plane]))
-        writes[-1].start()
-    for write in writes:
-        write.wait()
 
 
 def project_kernel(data_ref, templates_ref, clean_ref, power_ref):
@@ -160,33 +189,8 @@
         power_ref[member] = power
 
 
-def interval_of(bounds_ref, segment):
-    at = segment * SEGLEN
-    first = jnp.int32(0)
-    end = jnp.int32(SAMPLES)
-    for t in range(1, INTERVALS):
-        bound = bounds_ref[t]
-        first = jnp.where(bound <= at, jnp.maximum(first, bound), first)
-        end = jnp.where(bound > at, jnp.minimum(end, bound), end)
-    return first // SEGLEN, end // SEGLEN
-
-
-def prepare_kernel(
-    segment_ref, bounds_ref, index_ref, slot_ref, hot_ref, weight_ref, beyond_ref, share_ref
-):
+def slot_kernel(segment_ref, index_ref, slot_ref, hot_ref):
     segment = segment_ref[0]
-    base = segment // PLANE * PLANE
-    late = (segment & GROUP) != 0
-    first, end = interval_of(bounds_ref, segment)
-    part = 1.0 / jnp.full((8, SEGLEN), (end - first) * SEGLEN, jnp.int32).astype(f32)
-    share_ref[...] = jnp.where(jnp.where(late, end > base + PLANE, first < base), part, 0.0)
-    next_first, next_end = interval_of(bounds_ref, jnp.where(late, base + PLANE, base - 1))
-    edge = jnp.where(late, base + PLANE == SEGMENTS, base == 0)
-    next_first = jnp.where(edge, next_end, next_first)
-    for member in range(PLANE):
-        at = base + member
-        weight_ref[member] = jnp.where((at >= first) & (at < end), part, 0.0)
-        beyond_ref[member] = jnp.full((8, SEGLEN), jnp.where((at >= next_first) & (at < next_end), 1.0, 0.0), f32)
     pick = lax.broadcasted_iota(jnp.int32, (8, SEGMENTS), 1) == segment
     index = index_ref[...].astype(f32).astype(bf16)
     seen = lax.dot_general(
@@ -239,15 +243,15 @@
 HBM = pl.BlockSpec(memory_space=pltpu.HBM)
 
 
-def call(kernel, specs, outs, name, scratch=(), mib=16, out_spec=VMEM):
-    shapes = [jax.ShapeDtypeStruct(shape, dtype) for shape, dtype in outs]
+def call(kernel, specs, outs, name, scratch=()):
+    shapes = [pltpu.VMEM(shape, dtype) for shape, dtype in outs]
     return pl.pallas_call(
         kernel,
         out_shape=shapes if len(shapes) > 1 else shapes[0],
         in_specs=specs,
-        out_specs=[out_spec] * len(shapes) if len(shapes) > 1 else out_spec,
+        out_specs=[VMEM] * len(shapes) if len(shapes) > 1 else VMEM,
         scratch_shapes=list(scratch),
-        compiler_params=pltpu.CompilerParams(vmem_limit_bytes=mib * 1024 * 1024),
+        compiler_params=pltpu.CompilerParams(vmem_limit_bytes=16 * 1024 * 1024),
         name=name,
     )
 
@@ -265,31 +269,32 @@
     group = lax.rem(lax.axis_index("z") + core, PLANES)
     segment = (PLANE * group + GROUP * (1 - core) + lax.axis_index(("y", "x"))).astype(jnp.int32).reshape(1)
     rows = timelines.reshape(OWN_DETS, SEGMENTS, SEGLEN).transpose(1, 0, 2).reshape(DETS, SEGLEN)
-    scratch = [pltpu.SMEM((OWN_DETS,), f32)] * 3 + [
+    scratch = [pltpu.SMEM((INTERVALS + 1,), jnp.int32)] + [pltpu.SMEM((OWN_DETS,), f32)] * 3 + [
         pltpu.VMEM((DETS, SEGLEN), f32),
         pltpu.VMEM((2, SEGMENTS, SEGMENTS), bf16),
         pltpu.VMEM((2, SEGMENTS, SEGMENTS), bf16),
+        pltpu.VMEM((2, SEGMENTS, SEGMENTS), bf16),
         pltpu.VMEM((3, ROWS, SEGLEN), f32),
-        pltpu.VMEM((DETS, SEGLEN), f32),
-        pltpu.SemaphoreType.DMA((7,)),
-        pltpu.SemaphoreType.DMA((PLANES,)),
+        pltpu.SemaphoreType.DMA((9,)),
     ]
-    weighted = call(weight_kernel, [HBM] * 6, [((DETS, SEGLEN), f32)], "weight", scratch, 60, HBM)(
-        knee_freq, noise_slope, noise_level, rows, *[jnp.asarray(t) for t in tables()]
-    )
+    stored = [interval_bounds, knee_freq, noise_slope, noise_level, rows, *[jnp.asarray(t) for t in tables()]]
+    line, lines = ((8, SEGLEN), f32), ((PLANE, 8, SEGLEN), f32)
+    weighted, inside, outside, share = call(
+        weight_kernel, [HBM] * 7, [((DETS, SEGLEN), f32), lines, lines, line], "weight", scratch
+    )(*[pltpu.with_memory_space_constraint(array, pltpu.HBM) for array in stored])
     data = lax.all_to_all(
         weighted.reshape(SEGMENTS, OWN_DETS, SEGLEN), ALL, split_axis=0, concat_axis=0, tiled=True
     ).reshape(DETS, SEGLEN)
-    line, lines = ((8, SEGLEN), f32), ((PLANE, 8, SEGLEN), f32)
     cleaned, power = call(project_kernel, [VMEM] * 2, [((SEGLEN, DETS), f32), lines], "project")(data, templates)
     gathered = lax.all_to_all(
         power, ALL, split_axis=0, concat_axis=0, axis_index_groups=interval_groups(), tiled=True
     )
-    hot, inside, outside, share = call(
-        prepare_kernel, [SMEM] * 2 + [VMEM] * 2, [((BLOCKS, DETS), bf16), lines, lines, line], "prepare"
-    )(segment, interval_bounds, block_index, block_slot.reshape(1, BLOCKS))
     own, message = call(halo_kernel, [VMEM] * 3, [line] * 2, "halo")(gathered, inside, outside)
+    message, block_index = lax.optimization_barrier((message, block_index))
     beyond = lax.ppermute(message, "c", [(0, 1), (1, 0)])
+    hot = call(slot_kernel, [SMEM] + [VMEM] * 2, [((BLOCKS, DETS), bf16)], "slots")(
+        segment, block_index, block_slot.reshape(1, BLOCKS)
+    )
     partial = call(bin_kernel, [VMEM] * 5, [((BLOCKS, SEGLEN), f32)], "bin")(cleaned, own, share, beyond, hot)
     spread = lax.all_to_all(
         partial.reshape(32, 8, SEGLEN), ("y", "x", "c"), split_axis=0, concat_axis=0, tiled=True

time: 83.7 us -> 81.4 us (0.973)
  blocking collectives: 60.4 us -> 73.5 us
  waiting for transfers between devices: 8.01 us -> 0.35 us
  starting transfers between devices: 6.48 us -> 1.16 us
  Pallas kernels: 7.82 us -> 5.43 us
    all_to_all x0 -> x1, blocking collectives: none -> 13.4 us  [local(): lax.all_to_all(power, ALL, split_axis=0, concat_axis=0, axis_index_groups...]
    all_to_all x1 -> x0, waiting for transfers between devices: 7.18 us -> none  [local(): lax.all_to_all(power, ALL, split_axis=0, concat_axis=0, axis_index_groups...]
    all_to_all x1 -> x0, starting transfers between devices: 5.31 us -> none  [local(): lax.all_to_all(power, ALL, split_axis=0, concat_axis=0, axis_index_groups...]
    pallas_call x2, Pallas kernels: 4.9 us -> 3.59 us  [the longest x1 3.14 us: local(): call(weight_kernel, [HBM] * 7, [((DETS, SEGLEN), f32), lines, lines, line...]
    pallas_call x1, Pallas kernels: 2.4 us -> 1.31 us  [local(): call(project_kernel, [VMEM] * 2, [((SEGLEN, DETS), f32), lines], 'project')]
  transfers between devices with their start and end apart: 2 -> 1, of which waited for: 2 -> 1; matrix products, arithmetic and copies ran while one was open for 0% -> 0% of each run, Pallas kernels for 1% -> 1%
where the time goes in v4:
time: 81.4 us; the launch traced here: 81.2 us
  blocking collectives  73.5 us (90%)
  Pallas kernels  5.43 us (7%)
  starting transfers between devices  1.16 us (1%)
    all_to_all x1, blocking collectives, local(): lax.all_to_all(weighted.reshape(SEGMENTS, OWN_DETS, SEGLEN), ALL, split_a...  35.4 us
    all_to_all x1, blocking collectives, local(): lax.all_to_all(copies, ('z', 'y'), split_axis=0, concat_axis=0, tiled=True)  13.8 us
    all_to_all x1, blocking collectives, local(): lax.all_to_all(power, ALL, split_axis=0, concat_axis=0, axis_index_groups...  13.4 us
    all_to_all x1, blocking collectives, local(): lax.all_to_all(partial.reshape(32, 8, SEGLEN), ('y', 'x', 'c'), split_axi...  11 us
    pallas_call x1, Pallas kernels, local(): call(weight_kernel, [HBM] * 7, [((DETS, SEGLEN), f32), lines, lines, line...  3.14 us
  transfers between devices with their start and end apart: 1, of which 1 were waited for; matrix products, arithmetic and copies ran while one was open for 0% of the time, Pallas kernels for 1%

profile of v4, /device:TPU:1, one launch (start us, length us, event | category | flops | bytes accessed | tf_op | source)
XLA Modules:
  0.0 81.2 jit_solution(14933683403174639369)
XLA Ops:
  0.0 0.0 copy-start
  0.0 3.1 %weight.1 = (f32[1024,128]{1,0:T(8,128)S(1)}, f32[32,8,128]{2,1,0:T(8,128)S(1)}, f32[32,8,128]{2,1,0:T(8,128)S(1)}, f32[8,128]{1,0:T(8,128)S(1)}) custom-call(s32[33]{0:T(128)} %bounds_hbm.1, f32[4]{0:T(128)} %knee_hbm.1, f32[4]{0:T(128)} %slope_hbm.1, f32[4]{0:T(128)} %level_hbm.1, f32[1024,128]{1,0:T(8,128)} %bitcast.17, ...), custom_call_target="tpu_custom_call" | custom-call | tf_op jit(solution)/shard_map/weight/pallas_call | solution.py:282
  3.1 0.0 copy-start.1
  3.2 0.0 copy-start.2
  3.2 35.4 %all_to_all.20 = f32[256,4,128]{2,1,0:T(4,128)S(1)} all-to-all(f32[256,4,128]{2,1,0:T(4,128)S(1)} %bitcast.15), channel_id=1, replica_groups=mesh['z'=8,'y'=4,'x'=4,'c'=2] {'z','y','x','c'}, dimensions={0} | all-to-all | bytes 1048576 | tf_op jit(solution)/shard_map/all_to_all | solution.py:285
  38.5 0.0 copy-done
  38.5 1.3 %project.1 = (f32[128,1024]{1,0:T(8,128)S(1)}, f32[32,8,128]{2,1,0:T(8,128)S(1)}) custom-call(f32[1024,128]{1,0:T(8,128)S(1)} %bitcast.13, f32[1024,512]{1,0:T(8,128)S(1)} %copy-done), custom_call_target="tpu_custom_call" | custom-call | tf_op jit(solution)/shard_map/project/pallas_call | solution.py:288
  39.8 13.4 %all_to_all.21.gathered_ref = f32[32,8,128]{2,1,0:T(8,128)S(1)} all-to-all(f32[32,8,128]{2,1,0:T(8,128)S(1)} %get-tuple-element.17), channel_id=1, replica_groups={{225,227,229,231,233,235,237,239,241,243,245,247,249,251,253,255,0,2,4,..., dimensions={0} | all-to-all | bytes 262144 | tf_op jit(solution)/shard_map/all_to_all | solution.py:289
  53.2 1.2 %collective-permute-start = (f32[8,128]{1,0:T(8,128)S(1)}, f32[8,128]{1,0:T(8,128)S(1)}, u32[]{:S(2)}, u32[]{:S(2)}) collective-permute-start(f32[8,128]{1,0:T(8,128)S(1)} %get-tuple-element.23), channel_id=1, source_target_pairs={{0,1},{1,0},{2,3},{3,2},{4,5},{5,4},{6,7},{7,6},{8,9},{9,8},{10,11... | collective-permute-start | bytes 12296 | tf_op jit(solution)/shard_map/ppermute | solution.py:294
  54.4 0.0 copy-done.1
  54.4 0.0 copy-done.2
  54.4 0.5 slots.1.hot_ref
  54.9 0.4 collective-permute-done.message_ref
  55.2 0.4 bin.1
  55.7 11.0 %all_to_all.22.parts_ref = f32[32,8,128]{2,1,0:T(8,128)S(1)} all-to-all(f32[32,8,128]{2,1,0:T(8,128)S(1)} %bitcast.14), channel_id=1, replica_groups=mesh['z'=8,'y'=4,'x'=4,'c'=2] {'y','x','c'}, dimensions={0} | all-to-all | bytes 262144 | tf_op jit(solution)/shard_map/all_to_all | solution.py:299
  66.8 13.8 %all_to_all.23 = f32[32,8,128]{2,1,0:T(8,128)S(1)} all-to-all(f32[32,8,128]{2,1,0:T(8,128)S(1)} %fold.1), channel_id=1, replica_groups=mesh['z'=8,'y'=4,'x'=4,'c'=2] {'z','y'}, dimensions={0} | all-to-all | bytes 262144 | tf_op jit(solution)/shard_map/all_to_all | solution.py:303
  80.5 0.6 bitcast_reduce_fusion
  (2 shorter events, 0.1 us)
Async XLA Ops:
  0.0 38.5 %copy-start = (f32[1024,512]{1,0:T(8,128)S(1)}, f32[1024,512]{1,0:T(8,128)}, u32[]{:S(2)}) copy-start(f32[1024,512]{1,0:T(8,128)} %templates_ref.1) | copy-start | bytes 6291460
  3.1 51.3 %copy-start.1 = (s32[1024,256]{1,0:T(8,128)S(1)}, s32[1024,256]{1,0:T(8,128)}, u32[]{:S(2)}) copy-start(s32[1024,256]{1,0:T(8,128)} %index_ref) | copy-start | bytes 3145732
  3.2 51.3 %copy-start.2 = (s32[256]{0:T(256)S(1)}, s32[256]{0:T(256)}, u32[]{:S(2)}) copy-start(s32[256]{0:T(256)} %param.17) | copy-start | bytes 3076
  53.2 2.0 %collective-permute-start = (f32[8,128]{1,0:T(8,128)S(1)}, f32[8,128]{1,0:T(8,128)S(1)}, u32[]{:S(2)}, u32[]{:S(2)}) collective-permute-start(f32[8,128]{1,0:T(8,128)S(1)} %get-tuple-element.23), channel_id=1, source_target_pairs={{0,1},{1,0},{2,3},{3,2},{4,5},{5,4},{6,7},{7,6},{8,9},{9,8},{10,11... | collective-permute-start | bytes 12296 | tf_op jit(solution)/shard_map/ppermute | solution.py:294

commit v5 on v4

--- a/solution.py
+++ b/solution.py
@@ -29,9 +29,12 @@
 
 
 def split_np(table):
-    high = np.asarray(table, np.float32).astype(jnp.bfloat16)
-    low = (table - high.astype(np.float64)).astype(np.float32).astype(jnp.bfloat16)
-    return high, low
+    parts = []
+    rest = np.asarray(table, np.float64)
+    for _ in range(3):
+        parts.append(rest.astype(np.float32).astype(jnp.bfloat16))
+        rest = rest - parts[-1].astype(np.float64)
+    return parts
 
 
 def tables():
@@ -56,16 +59,21 @@
 
 def split(value):
     high = value.astype(bf16)
-    return high, (value - high.astype(f32)).astype(bf16)
-
-
-def dot3(a, b, dims):
-    def one(x, y):
-        return lax.dot_general(x, y, (dims, ((), ())), preferred_element_type=f32)
-
+    rest = value - high.astype(f32)
+    middle = rest.astype(bf16)
+    return high, middle, (rest - middle.astype(f32)).astype(bf16)
+
+
+def dot6(a, b, dims):
     rows = a[0].shape[0]
-    both = one(jnp.concatenate(a, axis=0), b[0])
-    return both[:rows] + (both[rows:] + one(a[0], b[1]))
+    total = None
+    for k in (2, 1, 0):
+        left = jnp.concatenate(a[: 3 - k], axis=0) if k < 2 else a[0]
+        product = lax.dot_general(left, b[k], (dims, ((), ())), preferred_element_type=f32)
+        for i in reversed(range(3 - k)):
+            part = product[rows * i : rows * (i + 1)]
+            total = part if total is None else total + part
+    return total
 
 
 NN = ((1,), (0,))
@@ -112,13 +120,13 @@
     pairs = [
         (bounds_hbm, bounds_ref),
         (x_hbm, x_ref),
-        (tables_hbm.at[pl.ds(0, 2)], outer_ref),
+        (tables_hbm.at[pl.ds(0, 3)], outer_ref),
         (factors_hbm, factors_ref),
-        (tables_hbm.at[pl.ds(2, 2)], inner_ref),
+        (tables_hbm.at[pl.ds(3, 3)], inner_ref),
         (knee_hbm, knee_ref),
         (slope_hbm, slope_ref),
         (level_hbm, level_ref),
-        (tables_hbm.at[pl.ds(4, 2)], back_ref),
+        (tables_hbm.at[pl.ds(6, 3)], back_ref),
     ]
     copies = [pltpu.make_async_copy(src, dst, sems.at[i]) for i, (src, dst) in enumerate(pairs)]
     for copy in copies:
@@ -128,12 +136,12 @@
     copies[1].wait()
     copies[2].wait()
     parts = [split(x_ref[pl.ds(d, SEGMENTS, stride=OWN_DETS), :]) for d in range(OWN_DETS)]
-    outer = (outer_ref[0], outer_ref[1])
-    samples = tuple(jnp.concatenate([part[i] for part in parts], axis=1) for i in range(2))
-    section = dot3(outer, samples, NN)
+    outer = (outer_ref[0], outer_ref[1], outer_ref[2])
+    samples = tuple(jnp.concatenate([part[i] for part in parts], axis=1) for i in range(3))
+    section = dot6(outer, samples, NN)
     for copy in copies[3:8]:
         copy.wait()
-    inner = (inner_ref[0], inner_ref[1])
+    inner = (inner_ref[0], inner_ref[1], inner_ref[2])
     cos, sin, log_fold = factors_ref[0], factors_ref[1], factors_ref[2]
     top = lax.broadcasted_iota(jnp.int32, (8, SEGLEN), 0) == 0
     stacked = []
@@ -143,7 +151,7 @@
         real = jnp.concatenate([real, jnp.where(top, imag[:8], 0.0)], axis=0)
         imag = jnp.concatenate([jnp.where(top, 0.0, imag[:8]), imag[8:], jnp.zeros((8, SEGLEN), f32)], axis=0)
         stacked.append(jnp.concatenate([real * cos + imag * sin, imag * cos - real * sin], axis=1))
-    spectrum = dot3(split(jnp.concatenate(stacked, axis=0)), inner, NN)
+    spectrum = dot6(split(jnp.concatenate(stacked, axis=0)), inner, NN)
     row = lax.broadcasted_iota(jnp.int32, (ROWS, SEGLEN), 0)
     zero_freq = (row == 0) & (lax.broadcasted_iota(jnp.int32, (ROWS, SEGLEN), 1) == 0)
     times = jnp.where((row == 0) | (row == HALF), 1.0 / SAMPLES, 2.0 / SAMPLES).astype(f32)
@@ -156,7 +164,7 @@
         weight = jnp.where(zero_freq, 0.0, times / ((1.0 + ratio) * (level * level)))
         part = spectrum[ROWS * d : ROWS * (d + 1)]
         shaped.append(part * jnp.concatenate([weight, weight], axis=1))
-    back = dot3(split(jnp.concatenate(shaped, axis=0)), inner, NT)
+    back = dot6(split(jnp.concatenate(shaped, axis=0)), inner, NT)
     turned = []
     for d in range(OWN_DETS):
         part = back[ROWS * d : ROWS * (d + 1)]
@@ -166,7 +174,7 @@
         first = jnp.where(top, jnp.broadcast_to(turn_re[HALF : HALF + 1], (8, SEGLEN)), turn_im[:8])
         turned.append(jnp.concatenate([turn_re[:HALF], first, turn_im[8:HALF]], axis=0))
     copies[8].wait()
-    result = dot3((back_ref[0], back_ref[1]), split(jnp.concatenate(turned, axis=1)), NN)
+    result = dot6((back_ref[0], back_ref[1], back_ref[2]), split(jnp.concatenate(turned, axis=1)), NN)
     for plane in range(PLANES):
         for core in range(2):
             start = held_at(plane, core)
@@ -180,8 +188,8 @@
 def project_kernel(data_ref, templates_ref, clean_ref, power_ref):
     data = data_ref[...].T
     pattern = split(templates_ref[...])
-    amplitudes = dot3(split(data), pattern, NN)
-    cleaned = data - dot3(split(amplitudes), pattern, NT)
+    amplitudes = dot6(split(data), pattern, NN)
+    cleaned = data - dot6(split(amplitudes), pattern, NT)
     clean_ref[...] = cleaned
     power = jnp.sum(cleaned * cleaned, axis=0, keepdims=True)
     power = jnp.concatenate([power[:, SEGLEN * k : SEGLEN * (k + 1)] for k in range(8)], axis=0)
@@ -222,11 +230,10 @@
     values = jnp.concatenate(
         [clean_ref[:, SEGLEN * k : SEGLEN * (k + 1)] * inverse[k : k + 1] for k in range(8)], axis=1
     )
-    high, low = split(values)
-    hot = hot_ref[...]
-    map_ref[...] = lax.dot_general(hot, high, (NT, ((), ())), preferred_element_type=f32) + lax.dot_general(
-        hot, low, (NT, ((), ())), preferred_element_type=f32
-    )
+    parts = lax.dot_general(
+        hot_ref[...], jnp.concatenate(split(values), axis=0), (NT, ((), ())), preferred_element_type=f32
+    )
+    map_ref[...] = parts[:, :SEGLEN] + (parts[:, SEGLEN : 2 * SEGLEN] + parts[:, 2 * SEGLEN :])
 
 
 def fold_kernel(parts_ref, out_ref):
@@ -271,9 +278,9 @@
     rows = timelines.reshape(OWN_DETS, SEGMENTS, SEGLEN).transpose(1, 0, 2).reshape(DETS, SEGLEN)
     scratch = [pltpu.SMEM((INTERVALS + 1,), jnp.int32)] + [pltpu.SMEM((OWN_DETS,), f32)] * 3 + [
         pltpu.VMEM((DETS, SEGLEN), f32),
-        pltpu.VMEM((2, SEGMENTS, SEGMENTS), bf16),
-        pltpu.VMEM((2, SEGMENTS, SEGMENTS), bf16),
-        pltpu.VMEM((2, SEGMENTS, SEGMENTS), bf16),
+        pltpu.VMEM((3, SEGMENTS, SEGMENTS), bf16),
+        pltpu.VMEM((3, SEGMENTS, SEGMENTS), bf16),
+        pltpu.VMEM((3, SEGMENTS, SEGMENTS), bf16),
         pltpu.VMEM((3, ROWS, SEGLEN), f32),
         pltpu.SemaphoreType.DMA((9,)),
     ]

time: 81.4 us -> 83.8 us (1.029)
  Pallas kernels: 5.43 us -> 7.84 us
    pallas_call x1, Pallas kernels: 3.14 us -> 4.51 us  [local(): call(weight_kernel, [HBM] * 7, [((DETS, SEGLEN), f32), lines, lines, line...]
    pallas_call x1, Pallas kernels: 1.31 us -> 2.32 us  [local(): call(project_kernel, [VMEM] * 2, [((SEGLEN, DETS), f32), lines], 'project')]
where the time goes in v5:
time: 83.8 us; the launch traced here: 83.5 us
  blocking collectives  73.5 us (88%)
  Pallas kernels  7.84 us (9%)
  starting transfers between devices  1.16 us (1%)
    all_to_all x1, blocking collectives, local(): lax.all_to_all(weighted.reshape(SEGMENTS, OWN_DETS, SEGLEN), ALL, split_a...  35.3 us
    all_to_all x1, blocking collectives, local(): lax.all_to_all(copies, ('z', 'y'), split_axis=0, concat_axis=0, tiled=True)  13.8 us
    all_to_all x1, blocking collectives, local(): lax.all_to_all(power, ALL, split_axis=0, concat_axis=0, axis_index_groups...  13.3 us
    all_to_all x1, blocking collectives, local(): lax.all_to_all(partial.reshape(32, 8, SEGLEN), ('y', 'x', 'c'), split_axi...  11 us
    pallas_call x1, Pallas kernels, local(): call(weight_kernel, [HBM] * 7, [((DETS, SEGLEN), f32), lines, lines, line...  4.51 us
    pallas_call x1, Pallas kernels, local(): call(project_kernel, [VMEM] * 2, [((SEGLEN, DETS), f32), lines], 'project')  2.32 us
  transfers between devices with their start and end apart: 1, of which 1 were waited for; matrix products, arithmetic and copies ran while one was open for 0% of the time, Pallas kernels for 1%

profile of v5, /device:TPU:1, one launch (start us, length us, event | category | flops | bytes accessed | tf_op | source)
XLA Modules:
  0.0 83.5 jit_solution(5832937128226629649)
XLA Ops:
  0.0 0.0 copy-start
  0.0 4.5 %weight.1 = (f32[1024,128]{1,0:T(8,128)S(1)}, f32[32,8,128]{2,1,0:T(8,128)S(1)}, f32[32,8,128]{2,1,0:T(8,128)S(1)}, f32[8,128]{1,0:T(8,128)S(1)}) custom-call(s32[33]{0:T(128)} %bounds_hbm.1, f32[4]{0:T(128)} %knee_hbm.1, f32[4]{0:T(128)} %slope_hbm.1, f32[4]{0:T(128)} %level_hbm.1, f32[1024,128]{1,0:T(8,128)} %bitcast.17, ...), custom_call_target="tpu_custom_call" | custom-call | tf_op jit(solution)/shard_map/weight/pallas_call | solution.py:289
  4.5 0.0 copy-start.1
  4.5 0.0 copy-start.2
  4.5 35.3 %all_to_all.20 = f32[256,4,128]{2,1,0:T(4,128)S(1)} all-to-all(f32[256,4,128]{2,1,0:T(4,128)S(1)} %bitcast.15), channel_id=1, replica_groups=mesh['z'=8,'y'=4,'x'=4,'c'=2] {'z','y','x','c'}, dimensions={0} | all-to-all | bytes 1048576 | tf_op jit(solution)/shard_map/all_to_all | solution.py:292
  39.9 0.0 copy-done
  39.9 2.3 %project.1 = (f32[128,1024]{1,0:T(8,128)S(1)}, f32[32,8,128]{2,1,0:T(8,128)S(1)}) custom-call(f32[1024,128]{1,0:T(8,128)S(1)} %bitcast.13, f32[1024,512]{1,0:T(8,128)S(1)} %copy-done), custom_call_target="tpu_custom_call" | custom-call | tf_op jit(solution)/shard_map/project/pallas_call | solution.py:295
  42.2 13.3 %all_to_all.21.gathered_ref = f32[32,8,128]{2,1,0:T(8,128)S(1)} all-to-all(f32[32,8,128]{2,1,0:T(8,128)S(1)} %get-tuple-element.17), channel_id=1, replica_groups={{225,227,229,231,233,235,237,239,241,243,245,247,249,251,253,255,0,2,4,..., dimensions={0} | all-to-all | bytes 262144 | tf_op jit(solution)/shard_map/all_to_all | solution.py:296
  55.6 1.2 %collective-permute-start = (f32[8,128]{1,0:T(8,128)S(1)}, f32[8,128]{1,0:T(8,128)S(1)}, u32[]{:S(2)}, u32[]{:S(2)}) collective-permute-start(f32[8,128]{1,0:T(8,128)S(1)} %get-tuple-element.23), channel_id=1, source_target_pairs={{0,1},{1,0},{2,3},{3,2},{4,5},{5,4},{6,7},{7,6},{8,9},{9,8},{10,11... | collective-permute-start | bytes 12296 | tf_op jit(solution)/shard_map/ppermute | solution.py:301
  56.8 0.0 copy-done.1
  56.8 0.0 copy-done.2
  56.8 0.5 slots.1.hot_ref
  57.2 0.4 collective-permute-done.message_ref
  57.6 0.5 bin.1
  58.1 11.0 %all_to_all.22.parts_ref = f32[32,8,128]{2,1,0:T(8,128)S(1)} all-to-all(f32[32,8,128]{2,1,0:T(8,128)S(1)} %bitcast.14), channel_id=1, replica_groups=mesh['z'=8,'y'=4,'x'=4,'c'=2] {'y','x','c'}, dimensions={0} | all-to-all | bytes 262144 | tf_op jit(solution)/shard_map/all_to_all | solution.py:306
  69.2 13.8 %all_to_all.23 = f32[32,8,128]{2,1,0:T(8,128)S(1)} all-to-all(f32[32,8,128]{2,1,0:T(8,128)S(1)} %fold.1), channel_id=1, replica_groups=mesh['z'=8,'y'=4,'x'=4,'c'=2] {'z','y'}, dimensions={0} | all-to-all | bytes 262144 | tf_op jit(solution)/shard_map/all_to_all | solution.py:310
  82.9 0.6 bitcast_reduce_fusion
  (2 shorter events, 0.1 us)
Async XLA Ops:
  0.0 39.9 %copy-start = (f32[1024,512]{1,0:T(8,128)S(1)}, f32[1024,512]{1,0:T(8,128)}, u32[]{:S(2)}) copy-start(f32[1024,512]{1,0:T(8,128)} %templates_ref.1) | copy-start | bytes 6291460
  4.5 52.3 %copy-start.1 = (s32[1024,256]{1,0:T(8,128)S(1)}, s32[1024,256]{1,0:T(8,128)}, u32[]{:S(2)}) copy-start(s32[1024,256]{1,0:T(8,128)} %index_ref) | copy-start | bytes 3145732
  4.5 52.2 %copy-start.2 = (s32[256]{0:T(256)S(1)}, s32[256]{0:T(256)}, u32[]{:S(2)}) copy-start(s32[256]{0:T(256)} %param.17) | copy-start | bytes 3076
  55.6 2.0 %collective-permute-start = (f32[8,128]{1,0:T(8,128)S(1)}, f32[8,128]{1,0:T(8,128)S(1)}, u32[]{:S(2)}, u32[]{:S(2)}) collective-permute-start(f32[8,128]{1,0:T(8,128)S(1)} %get-tuple-element.23), channel_id=1, source_target_pairs={{0,1},{1,0},{2,3},{3,2},{4,5},{5,4},{6,7},{7,6},{8,9},{9,8},{10,11... | collective-permute-start | bytes 12296 | tf_op jit(solution)/shard_map/ppermute | solution.py:301

commit v6 on v4

--- a/solution.py
+++ b/solution.py
@@ -222,11 +222,10 @@
     values = jnp.concatenate(
         [clean_ref[:, SEGLEN * k : SEGLEN * (k + 1)] * inverse[k : k + 1] for k in range(8)], axis=1
     )
-    high, low = split(values)
-    hot = hot_ref[...]
-    map_ref[...] = lax.dot_general(hot, high, (NT, ((), ())), preferred_element_type=f32) + lax.dot_general(
-        hot, low, (NT, ((), ())), preferred_element_type=f32
-    )
+    both = lax.dot_general(
+        hot_ref[...], jnp.concatenate(split(values), axis=0), (NT, ((), ())), preferred_element_type=f32
+    )
+    map_ref[...] = both[:, :SEGLEN] + both[:, SEGLEN:]
 
 
 def fold_kernel(parts_ref, out_ref):

time: 81.4 us -> 81.3 us (level)
  no operation moved by 1% of the time
where the time goes in v6:
time: 81.3 us; the launch traced here: 81.1 us
  blocking collectives  73.5 us (90%)
  Pallas kernels  5.34 us (7%)
  starting transfers between devices  1.16 us (1%)
    all_to_all x1, blocking collectives, local(): lax.all_to_all(weighted.reshape(SEGMENTS, OWN_DETS, SEGLEN), ALL, split_a...  35.4 us
    all_to_all x1, blocking collectives, local(): lax.all_to_all(copies, ('z', 'y'), split_axis=0, concat_axis=0, tiled=True)  13.8 us
    all_to_all x1, blocking collectives, local(): lax.all_to_all(power, ALL, split_axis=0, concat_axis=0, axis_index_groups...  13.4 us
    all_to_all x1, blocking collectives, local(): lax.all_to_all(partial.reshape(32, 8, SEGLEN), ('y', 'x', 'c'), split_axi...  11 us
    pallas_call x1, Pallas kernels, local(): call(weight_kernel, [HBM] * 7, [((DETS, SEGLEN), f32), lines, lines, line...  3.14 us
  transfers between devices with their start and end apart: 1, of which 1 were waited for; matrix products, arithmetic and copies ran while one was open for 0% of the time, Pallas kernels for 1%

profile of v6, /device:TPU:1, one launch (start us, length us, event | category | flops | bytes accessed | tf_op | source)
XLA Modules:
  0.0 81.1 jit_solution(10406790438985670352)
XLA Ops:
  0.0 0.0 copy-start
  0.0 3.1 %weight.1 = (f32[1024,128]{1,0:T(8,128)S(1)}, f32[32,8,128]{2,1,0:T(8,128)S(1)}, f32[32,8,128]{2,1,0:T(8,128)S(1)}, f32[8,128]{1,0:T(8,128)S(1)}) custom-call(s32[33]{0:T(128)} %bounds_hbm.1, f32[4]{0:T(128)} %knee_hbm.1, f32[4]{0:T(128)} %slope_hbm.1, f32[4]{0:T(128)} %level_hbm.1, f32[1024,128]{1,0:T(8,128)} %bitcast.17, ...), custom_call_target="tpu_custom_call" | custom-call | tf_op jit(solution)/shard_map/weight/pallas_call | solution.py:281
  3.1 0.0 copy-start.1
  3.2 0.0 copy-start.2
  3.2 35.4 %all_to_all.20 = f32[256,4,128]{2,1,0:T(4,128)S(1)} all-to-all(f32[256,4,128]{2,1,0:T(4,128)S(1)} %bitcast.15), channel_id=1, replica_groups=mesh['z'=8,'y'=4,'x'=4,'c'=2] {'z','y','x','c'}, dimensions={0} | all-to-all | bytes 1048576 | tf_op jit(solution)/shard_map/all_to_all | solution.py:284
  38.5 0.0 copy-done
  38.5 1.3 %project.1 = (f32[128,1024]{1,0:T(8,128)S(1)}, f32[32,8,128]{2,1,0:T(8,128)S(1)}) custom-call(f32[1024,128]{1,0:T(8,128)S(1)} %bitcast.13, f32[1024,512]{1,0:T(8,128)S(1)} %copy-done), custom_call_target="tpu_custom_call" | custom-call | tf_op jit(solution)/shard_map/project/pallas_call | solution.py:287
  39.8 13.4 %all_to_all.21.gathered_ref = f32[32,8,128]{2,1,0:T(8,128)S(1)} all-to-all(f32[32,8,128]{2,1,0:T(8,128)S(1)} %get-tuple-element.17), channel_id=1, replica_groups={{225,227,229,231,233,235,237,239,241,243,245,247,249,251,253,255,0,2,4,..., dimensions={0} | all-to-all | bytes 262144 | tf_op jit(solution)/shard_map/all_to_all | solution.py:288
  53.2 1.2 %collective-permute-start = (f32[8,128]{1,0:T(8,128)S(1)}, f32[8,128]{1,0:T(8,128)S(1)}, u32[]{:S(2)}, u32[]{:S(2)}) collective-permute-start(f32[8,128]{1,0:T(8,128)S(1)} %get-tuple-element.23), channel_id=1, source_target_pairs={{0,1},{1,0},{2,3},{3,2},{4,5},{5,4},{6,7},{7,6},{8,9},{9,8},{10,11... | collective-permute-start | bytes 12296 | tf_op jit(solution)/shard_map/ppermute | solution.py:293
  54.4 0.0 copy-done.1
  54.4 0.0 copy-done.2
  54.4 0.5 slots.1.hot_ref
  54.9 0.4 collective-permute-done.message_ref
  55.2 0.4 bin.1
  55.6 11.0 %all_to_all.22.parts_ref = f32[32,8,128]{2,1,0:T(8,128)S(1)} all-to-all(f32[32,8,128]{2,1,0:T(8,128)S(1)} %bitcast.14), channel_id=1, replica_groups=mesh['z'=8,'y'=4,'x'=4,'c'=2] {'y','x','c'}, dimensions={0} | all-to-all | bytes 262144 | tf_op jit(solution)/shard_map/all_to_all | solution.py:298
  66.7 13.8 %all_to_all.23 = f32[32,8,128]{2,1,0:T(8,128)S(1)} all-to-all(f32[32,8,128]{2,1,0:T(8,128)S(1)} %fold.1), channel_id=1, replica_groups=mesh['z'=8,'y'=4,'x'=4,'c'=2] {'z','y'}, dimensions={0} | all-to-all | bytes 262144 | tf_op jit(solution)/shard_map/all_to_all | solution.py:302
  80.4 0.6 bitcast_reduce_fusion
  (2 shorter events, 0.1 us)
Async XLA Ops:
  0.0 38.5 %copy-start = (f32[1024,512]{1,0:T(8,128)S(1)}, f32[1024,512]{1,0:T(8,128)}, u32[]{:S(2)}) copy-start(f32[1024,512]{1,0:T(8,128)} %templates_ref.1) | copy-start | bytes 6291460
  3.1 51.3 %copy-start.1 = (s32[1024,256]{1,0:T(8,128)S(1)}, s32[1024,256]{1,0:T(8,128)}, u32[]{:S(2)}) copy-start(s32[1024,256]{1,0:T(8,128)} %index_ref) | copy-start | bytes 3145732
  3.2 51.3 %copy-start.2 = (s32[256]{0:T(256)S(1)}, s32[256]{0:T(256)}, u32[]{:S(2)}) copy-start(s32[256]{0:T(256)} %param.17) | copy-start | bytes 3076
  53.2 2.0 %collective-permute-start = (f32[8,128]{1,0:T(8,128)S(1)}, f32[8,128]{1,0:T(8,128)S(1)}, u32[]{:S(2)}, u32[]{:S(2)}) collective-permute-start(f32[8,128]{1,0:T(8,128)S(1)} %get-tuple-element.23), channel_id=1, source_target_pairs={{0,1},{1,0},{2,3},{3,2},{4,5},{5,4},{6,7},{7,6},{8,9},{9,8},{10,11... | collective-permute-start | bytes 12296 | tf_op jit(solution)/shard_map/ppermute | solution.py:293

commit v7 on v6

--- a/solution.py
+++ b/solution.py
@@ -200,7 +200,7 @@
     hot = jnp.where(jnp.broadcast_to(seen[0:1].astype(jnp.int32), (BLOCKS, DETS)) == block, 1.0, 0.0).astype(bf16)
     table = jnp.broadcast_to(slot_ref[...].astype(f32).astype(bf16), (8, BLOCKS))
     slot = lax.dot_general(table, hot, (NN, ((), ())), preferred_element_type=f32)
-    row = ((block >> 3) & 7) * 32 + (block >> 6) * 8 + (block & 7)
+    row = ((block >> 4) & 7) * 32 + (block >> 7) * 16 + (block & 15)
     hot_ref[...] = jnp.where(
         jnp.broadcast_to(slot[0:1].astype(jnp.int32), (BLOCKS, DETS)) == row, 1.0, 0.0
     ).astype(bf16)
@@ -230,10 +230,14 @@
 
 def fold_kernel(parts_ref, out_ref):
     total = parts_ref[0]
-    for i in range(1, parts_ref.shape[0]):
+    for i in range(1, GROUP):
         total = total + parts_ref[i]
-    total = total * MAP_SCALE
-    for i in range(out_ref.shape[0]):
+    out_ref[...] = total * MAP_SCALE
+
+
+def copy_kernel(own_ref, other_ref, out_ref):
+    total = own_ref[...] + other_ref[...]
+    for i in range(GROUP):
         out_ref[i] = total
 
 
@@ -260,6 +264,16 @@
     for k in range(PLANES):
         early = [PLANE * ((k - 1) % PLANES) + 2 * m + 1 for m in range(GROUP)]
         groups.append(early + [PLANE * k + 2 * m for m in range(GROUP)])
+    return groups
+
+
+def half_groups(before, after):
+    groups = []
+    for outer in range(2):
+        order = [3 * outer, 3 * outer + 1 - 2 * outer]
+        groups.append(
+            [(b * 4 + y) * len(after) + a for b in before for y in order for a in after]
+        )
     return groups
 
 
@@ -296,10 +310,16 @@
     )
     partial = call(bin_kernel, [VMEM] * 5, [((BLOCKS, SEGLEN), f32)], "bin")(cleaned, own, share, beyond, hot)
     spread = lax.all_to_all(
-        partial.reshape(32, 8, SEGLEN), ("y", "x", "c"), split_axis=0, concat_axis=0, tiled=True
-    )
-    copies = call(fold_kernel, [VMEM], [((32, 8, SEGLEN), f32)], "fold")(spread)
-    sums = lax.all_to_all(copies, ("z", "y"), split_axis=0, concat_axis=0, tiled=True)
+        partial.reshape(GROUP, GROUP, SEGLEN), ("y", "x", "c"), split_axis=0, concat_axis=0,
+        axis_index_groups=half_groups(range(1), range(8)), tiled=True,
+    )
+    half = call(fold_kernel, [VMEM], [((GROUP, SEGLEN), f32)], "fold")(spread)
+    mirror = lax.ppermute(half, "y", [(i, 3 - i) for i in range(4)])
+    copies = call(copy_kernel, [VMEM] * 2, [((GROUP, GROUP, SEGLEN), f32)], "copies")(half, mirror)
+    sums = lax.all_to_all(
+        copies, ("z", "y"), split_axis=0, concat_axis=0,
+        axis_index_groups=half_groups(range(PLANES), range(1)), tiled=True,
+    )
     return jnp.sum(sums.reshape(8, 32, SEGLEN), axis=0)
 
 

time: 81.3 us -> 81.5 us (level)
  blocking collectives: 73.5 us -> 69.3 us
  waiting for transfers between devices: 0.35 us -> 3.19 us
  starting transfers between devices: 1.16 us -> 2.12 us
    all_to_all x2, blocking collectives: 24.8 us -> 20.6 us  [the longest x1 11.7 us: local(): lax.all_to_all(copies, ('z', 'y'), split_axis=0, concat_axis=0, axis_inde...]
    ppermute x0 -> x1, waiting for transfers between devices: none -> 2.84 us  [local(): mirror = lax.ppermute(half, 'y', [(i, 3 - i) for i in range(4)])]
    ppermute x0 -> x1, starting transfers between devices: none -> 0.96 us  [local(): mirror = lax.ppermute(half, 'y', [(i, 3 - i) for i in range(4)])]
  transfers between devices with their start and end apart: 1 -> 2, of which waited for: 1 -> 2; matrix products, arithmetic and copies ran while one was open for 0% -> 0% of each run, Pallas kernels for 1% -> 1%
where the time goes in v7:
time: 81.5 us; the launch traced here: 80.6 us
  blocking collectives  69.3 us (85%)
  Pallas kernels  5.32 us (7%)
  waiting for transfers between devices  3.19 us (4%)
  starting transfers between devices  2.12 us (3%)
    all_to_all x1, blocking collectives, local(): lax.all_to_all(weighted.reshape(SEGMENTS, OWN_DETS, SEGLEN), ALL, split_a...  35.4 us
    all_to_all x1, blocking collectives, local(): lax.all_to_all(power, ALL, split_axis=0, concat_axis=0, axis_index_groups...  13.4 us
    all_to_all x1, blocking collectives, local(): lax.all_to_all(copies, ('z', 'y'), split_axis=0, concat_axis=0, axis_inde...  11.7 us
    all_to_all x1, blocking collectives, local(): lax.all_to_all(partial.reshape(GROUP, GROUP, SEGLEN), ('y', 'x', 'c'), sp...  8.9 us
    pallas_call x1, Pallas kernels, local(): call(weight_kernel, [HBM] * 7, [((DETS, SEGLEN), f32), lines, lines, line...  3.14 us
    ppermute x1, waiting for transfers between devices, local(): mirror = lax.ppermute(half, 'y', [(i, 3 - i) for i in range(4)])  2.84 us
  transfers between devices with their start and end apart: 2, of which 2 were waited for; matrix products, arithmetic and copies ran while one was open for 0% of the time, Pallas kernels for 1%

profile of v7, /device:TPU:1, one launch (start us, length us, event | category | flops | bytes accessed | tf_op | source)
XLA Modules:
  0.0 80.6 jit_solution(4552279565110694531)
XLA Ops:
  0.0 0.0 copy-start
  0.0 3.1 %weight.1 = (f32[1024,128]{1,0:T(8,128)S(1)}, f32[32,8,128]{2,1,0:T(8,128)S(1)}, f32[32,8,128]{2,1,0:T(8,128)S(1)}, f32[8,128]{1,0:T(8,128)S(1)}) custom-call(s32[33]{0:T(128)} %bounds_hbm.1, f32[4]{0:T(128)} %knee_hbm.1, f32[4]{0:T(128)} %slope_hbm.1, f32[4]{0:T(128)} %level_hbm.1, f32[1024,128]{1,0:T(8,128)} %bitcast.17, ...), custom_call_target="tpu_custom_call" | custom-call | tf_op jit(solution)/shard_map/weight/pallas_call | solution.py:295
  3.1 0.0 copy-start.1
  3.2 0.0 copy-start.2
  3.2 35.4 %all_to_all.20 = f32[256,4,128]{2,1,0:T(4,128)S(1)} all-to-all(f32[256,4,128]{2,1,0:T(4,128)S(1)} %bitcast.15), channel_id=1, replica_groups=mesh['z'=8,'y'=4,'x'=4,'c'=2] {'z','y','x','c'}, dimensions={0} | all-to-all | bytes 1048576 | tf_op jit(solution)/shard_map/all_to_all | solution.py:298
  38.5 0.0 copy-done
  38.5 1.3 %project.1 = (f32[128,1024]{1,0:T(8,128)S(1)}, f32[32,8,128]{2,1,0:T(8,128)S(1)}) custom-call(f32[1024,128]{1,0:T(8,128)S(1)} %bitcast.13, f32[1024,512]{1,0:T(8,128)S(1)} %copy-done), custom_call_target="tpu_custom_call" | custom-call | tf_op jit(solution)/shard_map/project/pallas_call | solution.py:301
  39.8 13.4 %all_to_all.21.gathered_ref = f32[32,8,128]{2,1,0:T(8,128)S(1)} all-to-all(f32[32,8,128]{2,1,0:T(8,128)S(1)} %get-tuple-element.17), channel_id=1, replica_groups={{225,227,229,231,233,235,237,239,241,243,245,247,249,251,253,255,0,2,4,..., dimensions={0} | all-to-all | bytes 262144 | tf_op jit(solution)/shard_map/all_to_all | solution.py:302
  53.2 1.2 %collective-permute-start = (f32[8,128]{1,0:T(8,128)S(1)}, f32[8,128]{1,0:T(8,128)S(1)}, u32[]{:S(2)}, u32[]{:S(2)}) collective-permute-start(f32[8,128]{1,0:T(8,128)S(1)} %get-tuple-element.23), channel_id=1, source_target_pairs={{0,1},{1,0},{2,3},{3,2},{4,5},{5,4},{6,7},{7,6},{8,9},{9,8},{10,11... | collective-permute-start | bytes 12296 | tf_op jit(solution)/shard_map/ppermute | solution.py:307
  54.4 0.0 copy-done.1
  54.4 0.0 copy-done.2
  54.4 0.5 slots.1.hot_ref
  54.9 0.4 collective-permute-done.message_ref
  55.2 0.4 bin.1
  55.6 8.9 %all_to_all.22.parts_ref = f32[16,16,128]{2,1,0:T(8,128)S(1)} all-to-all(f32[16,16,128]{2,1,0:T(8,128)S(1)} %bitcast.14), channel_id=1, replica_groups={{0,1,2,3,4,5,6,7,8,9,10,11,12,13,14,15},{24,25,26,27,28,29,30,31,16,17,..., dimensions={0} | all-to-all | bytes 262144 | tf_op jit(solution)/shard_map/all_to_all | solution.py:312
  64.5 1.0 %collective-permute-start.1 = (f32[16,128]{1,0:T(8,128)S(1)}, f32[16,128]{1,0:T(8,128)S(1)}, u32[]{:S(2)}, u32[]{:S(2)}) collective-permute-start(f32[16,128]{1,0:T(8,128)S(1)} %fold.1.own_ref), channel_id=1, source_target_pairs={{0,24},{8,16},{16,8},{24,0},{1,25},{9,17},{17,9},{25,1},{2,26},{10... | collective-permute-start | bytes 24584 | tf_op jit(solution)/shard_map/ppermute | solution.py:317
  65.5 2.8 %collective-permute-done.1.other_ref = f32[16,128]{1,0:T(8,128)S(1)} collective-permute-done((f32[16,128]{1,0:T(8,128)S(1)}, f32[16,128]{1,0:T(8,128)S(1)}, u32[]{:S(2)}, u32[]{:S(2)}) %collective-permute-start.1) | collective-permute-done | bytes 8224 | tf_op jit(solution)/shard_map/ppermute | solution.py:317
  68.3 11.7 %all_to_all.23 = f32[16,16,128]{2,1,0:T(8,128)S(1)} all-to-all(f32[16,16,128]{2,1,0:T(8,128)S(1)} %copies.1), channel_id=1, replica_groups={{0,8,32,40,64,72,96,104,128,136,160,168,192,200,224,232},{24,16,56,48,8..., dimensions={0} | all-to-all | bytes 262144 | tf_op jit(solution)/shard_map/all_to_all | solution.py:319
  80.0 0.6 bitcast_reduce_fusion
  (3 shorter events, 0.1 us)
Async XLA Ops:
  0.0 38.5 %copy-start = (f32[1024,512]{1,0:T(8,128)S(1)}, f32[1024,512]{1,0:T(8,128)}, u32[]{:S(2)}) copy-start(f32[1024,512]{1,0:T(8,128)} %templates_ref.1) | copy-start | bytes 6291460
  3.1 51.3 %copy-start.1 = (s32[1024,256]{1,0:T(8,128)S(1)}, s32[1024,256]{1,0:T(8,128)}, u32[]{:S(2)}) copy-start(s32[1024,256]{1,0:T(8,128)} %index_ref) | copy-start | bytes 3145732
  3.2 51.3 %copy-start.2 = (s32[256]{0:T(256)S(1)}, s32[256]{0:T(256)}, u32[]{:S(2)}) copy-start(s32[256]{0:T(256)} %param.17) | copy-start | bytes 3076
  53.2 2.0 %collective-permute-start = (f32[8,128]{1,0:T(8,128)S(1)}, f32[8,128]{1,0:T(8,128)S(1)}, u32[]{:S(2)}, u32[]{:S(2)}) collective-permute-start(f32[8,128]{1,0:T(8,128)S(1)} %get-tuple-element.23), channel_id=1, source_target_pairs={{0,1},{1,0},{2,3},{3,2},{4,5},{5,4},{6,7},{7,6},{8,9},{9,8},{10,11... | collective-permute-start | bytes 12296 | tf_op jit(solution)/shard_map/ppermute | solution.py:307
  64.5 3.8 %collective-permute-start.1 = (f32[16,128]{1,0:T(8,128)S(1)}, f32[16,128]{1,0:T(8,128)S(1)}, u32[]{:S(2)}, u32[]{:S(2)}) collective-permute-start(f32[16,128]{1,0:T(8,128)S(1)} %fold.1.own_ref), channel_id=1, source_target_pairs={{0,24},{8,16},{16,8},{24,0},{1,25},{9,17},{17,9},{25,1},{2,26},{10... | collective-permute-start | bytes 24584 | tf_op jit(solution)/shard_map/ppermute | solution.py:317

commit v8 on v6

--- a/solution.py
+++ b/solution.py
@@ -72,8 +72,8 @@
 NT = ((1,), (1,))
 
 
-def held_at(plane, core):
-    return PLANE * ((plane + core) % PLANES) + GROUP * (1 - core)
+def held_at(plane, half):
+    return PLANE * plane + GROUP * (half ^ (plane & 1))
 
 
 def interval_of(bounds_ref, segment):
@@ -87,26 +87,31 @@
     return first // SEGLEN, end // SEGLEN
 
 
-def member_weights(bounds_ref, inside_ref, outside_ref, share_ref):
-    core = lax.axis_index("c")
-    base = PLANE * lax.rem(lax.axis_index("z") + core, PLANES)
-    segment = base + GROUP * (1 - core) + 4 * lax.axis_index("y") + lax.axis_index("x")
-    late = core == 0
+def member_weights(bounds_ref, inside_ref, near_ref, far_ref, share_ref):
+    z, y = lax.axis_index("z"), lax.axis_index("y")
+    odd = (y >> 1) ^ (z & 1)
+    base = PLANE * z + GROUP * odd
+    segment = base + 8 * (y & 1) + 2 * lax.axis_index("x") + lax.axis_index("c")
     first, end = interval_of(bounds_ref, segment)
     part = 1.0 / jnp.full((8, SEGLEN), (end - first) * SEGLEN, jnp.int32).astype(f32)
-    share_ref[...] = jnp.where(jnp.where(late, end > base + PLANE, first < base), part, 0.0)
-    next_first, next_end = interval_of(bounds_ref, jnp.where(late, base + PLANE, base - 1))
-    edge = jnp.where(late, base + PLANE == SEGMENTS, base == 0)
-    next_first = jnp.where(edge, next_end, next_first)
-    for member in range(PLANE):
+    for member in range(GROUP):
         at = base + member
         inside_ref[member] = jnp.where((at >= first) & (at < end), part, 0.0)
-        outside_ref[member] = jnp.full((8, SEGLEN), jnp.where((at >= next_first) & (at < next_end), 1.0, 0.0), f32)
+    for i, message_ref in ((0, near_ref), (1, far_ref)):
+        ahead = odd == i
+        share_ref[i] = jnp.where(jnp.where(ahead, end > base + GROUP, first < base), part, 0.0)
+        next_first, next_end = interval_of(bounds_ref, jnp.where(ahead, base + GROUP, base - 1))
+        edge = jnp.where(ahead, base + GROUP == SEGMENTS, base == 0)
+        next_first = jnp.where(edge, next_end, next_first)
+        for member in range(GROUP):
+            at = base + member
+            inside = (at >= next_first) & (at < next_end)
+            message_ref[member] = jnp.full((8, SEGLEN), jnp.where(inside, 1.0, 0.0), f32)
 
 
 def weight_kernel(
     bounds_hbm, knee_hbm, slope_hbm, level_hbm, x_hbm, tables_hbm, factors_hbm,
-    out_ref, inside_ref, outside_ref, share_ref,
+    out_ref, inside_ref, near_ref, far_ref, share_ref,
     bounds_ref, knee_ref, slope_ref, level_ref, x_ref, outer_ref, inner_ref, back_ref, factors_ref, sems,
 ):
     pairs = [
@@ -124,7 +129,7 @@
     for copy in copies:
         copy.start()
     copies[0].wait()
-    member_weights(bounds_ref, inside_ref, outside_ref, share_ref)
+    member_weights(bounds_ref, inside_ref, near_ref, far_ref, share_ref)
     copies[1].wait()
     copies[2].wait()
     parts = [split(x_ref[pl.ds(d, SEGMENTS, stride=OWN_DETS), :]) for d in range(OWN_DETS)]
@@ -168,11 +173,11 @@
     copies[8].wait()
     result = dot3((back_ref[0], back_ref[1]), split(jnp.concatenate(turned, axis=1)), NN)
     for plane in range(PLANES):
-        for core in range(2):
-            start = held_at(plane, core)
+        for side in range(2):
+            start = held_at(plane, side)
             for d in range(OWN_DETS):
-                row = (PLANE * plane + core) * OWN_DETS + d
-                out_ref[pl.ds(row, GROUP, stride=2 * OWN_DETS), :] = result[
+                row = (PLANE * plane + GROUP * side) * OWN_DETS + d
+                out_ref[pl.ds(row, GROUP, stride=OWN_DETS), :] = result[
                     start : start + GROUP, SEGLEN * d : SEGLEN * (d + 1)
                 ]
 
@@ -185,7 +190,7 @@
     clean_ref[...] = cleaned
     power = jnp.sum(cleaned * cleaned, axis=0, keepdims=True)
     power = jnp.concatenate([power[:, SEGLEN * k : SEGLEN * (k + 1)] for k in range(8)], axis=0)
-    for member in range(PLANE):
+    for member in range(GROUP):
         power_ref[member] = power
 
 
@@ -206,19 +211,22 @@
     ).astype(bf16)
 
 
-def halo_kernel(gathered_ref, weight_ref, beyond_ref, own_ref, message_ref):
+def halo_kernel(gathered_ref, inside_ref, near_ref, far_ref, own_ref, near_out, far_out):
     own = jnp.full((8, SEGLEN), EPS, f32)
-    message = jnp.zeros((8, SEGLEN), f32)
-    for member in range(PLANE):
+    near = jnp.zeros((8, SEGLEN), f32)
+    far = near
+    for member in range(GROUP):
         power = gathered_ref[member]
-        own = own + weight_ref[member] * power
-        message = message + beyond_ref[member] * power
+        own = own + inside_ref[member] * power
+        near = near + near_ref[member] * power
+        far = far + far_ref[member] * power
     own_ref[...] = own
-    message_ref[...] = message
-
-
-def bin_kernel(clean_ref, own_ref, share_ref, message_ref, hot_ref, map_ref):
-    inverse = 1.0 / (own_ref[...] + share_ref[...] * message_ref[...])
+    near_out[...] = near
+    far_out[...] = far
+
+
+def bin_kernel(clean_ref, own_ref, share_ref, near_ref, far_ref, hot_ref, map_ref):
+    inverse = 1.0 / (own_ref[...] + share_ref[0] * near_ref[...] + share_ref[1] * far_ref[...])
     values = jnp.concatenate(
         [clean_ref[:, SEGLEN * k : SEGLEN * (k + 1)] * inverse[k : k + 1] for k in range(8)], axis=1
     )
@@ -255,18 +263,19 @@
     )
 
 
-def interval_groups():
-    groups = []
-    for k in range(PLANES):
-        early = [PLANE * ((k - 1) % PLANES) + 2 * m + 1 for m in range(GROUP)]
-        groups.append(early + [PLANE * k + 2 * m for m in range(GROUP)])
-    return groups
+def far_pairs():
+    pairs = []
+    for z in range(PLANES):
+        for y in range(4):
+            z_to = z ^ 1 if y >> 1 else (z + (1 if z % 2 else -1)) % PLANES
+            pairs.append((4 * z + y, 4 * z_to + y))
+    return pairs
 
 
 def local(timelines, knee_freq, noise_slope, noise_level, templates, interval_bounds, block_index, block_slot):
-    core = lax.axis_index("c")
-    group = lax.rem(lax.axis_index("z") + core, PLANES)
-    segment = (PLANE * group + GROUP * (1 - core) + lax.axis_index(("y", "x"))).astype(jnp.int32).reshape(1)
+    z, y = lax.axis_index("z"), lax.axis_index("y")
+    base = PLANE * z + GROUP * ((y >> 1) ^ (z & 1))
+    segment = (base + 8 * (y & 1) + lax.axis_index(("x", "c"))).astype(jnp.int32).reshape(1)
     rows = timelines.reshape(OWN_DETS, SEGMENTS, SEGLEN).transpose(1, 0, 2).reshape(DETS, SEGLEN)
     scratch = [pltpu.SMEM((INTERVALS + 1,), jnp.int32)] + [pltpu.SMEM((OWN_DETS,), f32)] * 3 + [
         pltpu.VMEM((DETS, SEGLEN), f32),
@@ -277,24 +286,28 @@
         pltpu.SemaphoreType.DMA((9,)),
     ]
     stored = [interval_bounds, knee_freq, noise_slope, noise_level, rows, *[jnp.asarray(t) for t in tables()]]
-    line, lines = ((8, SEGLEN), f32), ((PLANE, 8, SEGLEN), f32)
-    weighted, inside, outside, share = call(
-        weight_kernel, [HBM] * 7, [((DETS, SEGLEN), f32), lines, lines, line], "weight", scratch
+    line, lines, two = [((*lead, 8, SEGLEN), f32) for lead in ((), (GROUP,), (2,))]
+    weighted, inside, to_near, to_far, share = call(
+        weight_kernel, [HBM] * 7, [((DETS, SEGLEN), f32), lines, lines, lines, two], "weight", scratch
     )(*[pltpu.with_memory_space_constraint(array, pltpu.HBM) for array in stored])
     data = lax.all_to_all(
         weighted.reshape(SEGMENTS, OWN_DETS, SEGLEN), ALL, split_axis=0, concat_axis=0, tiled=True
     ).reshape(DETS, SEGLEN)
     cleaned, power = call(project_kernel, [VMEM] * 2, [((SEGLEN, DETS), f32), lines], "project")(data, templates)
     gathered = lax.all_to_all(
-        power, ALL, split_axis=0, concat_axis=0, axis_index_groups=interval_groups(), tiled=True
-    )
-    own, message = call(halo_kernel, [VMEM] * 3, [line] * 2, "halo")(gathered, inside, outside)
-    message, block_index = lax.optimization_barrier((message, block_index))
-    beyond = lax.ppermute(message, "c", [(0, 1), (1, 0)])
+        power, ("y", "x", "c"), split_axis=0, concat_axis=0,
+        axis_index_groups=[list(range(16)), list(range(16, 32))], tiled=True,
+    )
+    own, near, far = call(halo_kernel, [VMEM] * 4, [line] * 3, "halo")(gathered, inside, to_near, to_far)
+    near, far, block_index = lax.optimization_barrier((near, far, block_index))
+    near = lax.ppermute(near, "y", [(i, 3 - i) for i in range(4)])
+    far = lax.ppermute(far, ("z", "y"), far_pairs())
     hot = call(slot_kernel, [SMEM] + [VMEM] * 2, [((BLOCKS, DETS), bf16)], "slots")(
         segment, block_index, block_slot.reshape(1, BLOCKS)
     )
-    partial = call(bin_kernel, [VMEM] * 5, [((BLOCKS, SEGLEN), f32)], "bin")(cleaned, own, share, beyond, hot)
+    partial = call(bin_kernel, [VMEM] * 6, [((BLOCKS, SEGLEN), f32)], "bin")(
+        cleaned, own, share, near, far, hot
+    )
     spread = lax.all_to_all(
         partial.reshape(32, 8, SEGLEN), ("y", "x", "c"), split_axis=0, concat_axis=0, tiled=True
     )

time: 81.3 us -> 80.7 us (level)
  blocking collectives: 73.5 us -> 70.9 us
  waiting for transfers between devices: 0.35 us -> 2.39 us
    all_to_all x1, blocking collectives: 13.4 us -> 10.4 us  [local(): lax.all_to_all(power, ('y', 'x', 'c'), split_axis=0, concat_axis=0, axis_...]
    ppermute x1 -> x2, waiting for transfers between devices: 0.35 us -> 2.39 us  [the longest x1 2.08 us: local(): near = lax.ppermute(near, 'y', [(i, 3 - i) for i in range(4)])]
    all_to_all x1, blocking collectives: 11 us -> 12.8 us  [local(): lax.all_to_all(partial.reshape(32, 8, SEGLEN), ('y', 'x', 'c'), split_axi...]
    all_to_all x1, blocking collectives: 13.8 us -> 12.3 us  [local(): lax.all_to_all(copies, ('z', 'y'), split_axis=0, concat_axis=0, tiled=True)]
  transfers between devices with their start and end apart: 1 -> 2, of which waited for: 1 -> 2; matrix products, arithmetic and copies ran while one was open for 0% -> 0% of each run, Pallas kernels for 1% -> 1%
where the time goes in v8:
time: 80.7 us; the launch traced here: 80.5 us
  blocking collectives  70.9 us (88%)
  Pallas kernels  5.29 us (7%)
  waiting for transfers between devices  2.39 us (3%)
  starting transfers between devices  1.2 us (1%)
    all_to_all x1, blocking collectives, local(): lax.all_to_all(weighted.reshape(SEGMENTS, OWN_DETS, SEGLEN), ALL, split_a...  35.4 us
    all_to_all x1, blocking collectives, local(): lax.all_to_all(partial.reshape(32, 8, SEGLEN), ('y', 'x', 'c'), split_axi...  12.8 us
    all_to_all x1, blocking collectives, local(): lax.all_to_all(copies, ('z', 'y'), split_axis=0, concat_axis=0, tiled=True)  12.3 us
    all_to_all x1, blocking collectives, local(): lax.all_to_all(power, ('y', 'x', 'c'), split_axis=0, concat_axis=0, axis_...  10.4 us
    pallas_call x1, Pallas kernels, local(): call(weight_kernel, [HBM] * 7, [((DETS, SEGLEN), f32), lines, lines, line...  3.1 us
    ppermute x1, waiting for transfers between devices, local(): near = lax.ppermute(near, 'y', [(i, 3 - i) for i in range(4)])  2.08 us
  transfers between devices with their start and end apart: 2, of which 2 were waited for; matrix products, arithmetic and copies ran while one was open for 0% of the time, Pallas kernels for 1%

profile of v8, /device:TPU:1, one launch (start us, length us, event | category | flops | bytes accessed | tf_op | source)
XLA Modules:
  0.0 80.5 jit_solution(159417541749183046)
XLA Ops:
  0.0 0.0 copy-start
  0.0 3.1 %weight.1 = (f32[1024,128]{1,0:T(8,128)S(1)}, f32[16,8,128]{2,1,0:T(8,128)S(1)}, f32[16,8,128]{2,1,0:T(8,128)S(1)}, f32[16,8,128]{2,1,0:T(8,128)S(1)}, f32[2,8,128]{2,1,0:T(8,128)S(1)}) custom-call(s32[33]{0:T(128)} %bounds_hbm.1, f32[4]{0:T(128)} %knee_hbm.1, f32[4]{0:T(128)} %slope_hbm.1, f32[4]{0:T(128)} %level_hbm.1, f32[1024,128]{1,0:T(8,128)} %bitcast.17, ...), custom_call_target="tpu_custom_call" | custom-call | tf_op jit(solution)/shard_map/weight/pallas_call | solution.py:290
  3.1 0.0 copy-start.1
  3.1 0.0 copy-start.2
  3.1 35.4 %all_to_all.20 = f32[256,4,128]{2,1,0:T(4,128)S(1)} all-to-all(f32[256,4,128]{2,1,0:T(4,128)S(1)} %bitcast.15), channel_id=1, replica_groups=mesh['z'=8,'y'=4,'x'=4,'c'=2] {'z','y','x','c'}, dimensions={0} | all-to-all | bytes 1048576 | tf_op jit(solution)/shard_map/all_to_all | solution.py:293
  38.5 0.0 copy-done
  38.5 1.3 %project.1 = (f32[128,1024]{1,0:T(8,128)S(1)}, f32[16,8,128]{2,1,0:T(8,128)S(1)}) custom-call(f32[1024,128]{1,0:T(8,128)S(1)} %bitcast.13, f32[1024,512]{1,0:T(8,128)S(1)} %copy-done), custom_call_target="tpu_custom_call" | custom-call | tf_op jit(solution)/shard_map/project/pallas_call | solution.py:296
  39.8 10.4 %all_to_all.21.gathered_ref = f32[16,8,128]{2,1,0:T(8,128)S(1)} all-to-all(f32[16,8,128]{2,1,0:T(8,128)S(1)} %get-tuple-element.20), channel_id=1, replica_groups={{0,1,2,3,4,5,6,7,8,9,10,11,12,13,14,15},{16,17,18,19,20,21,22,23,24,25,..., dimensions={0} | all-to-all | bytes 131072 | tf_op jit(solution)/shard_map/all_to_all | solution.py:297
  50.3 0.4 collective-permute-start
  50.7 0.8 collective-permute-start.1
  51.5 0.0 copy-done.1
  51.5 0.0 copy-done.2
  51.5 0.5 slots.1.hot_ref
  51.9 2.1 %collective-permute-done.near_ref = f32[8,128]{1,0:T(8,128)S(1)} collective-permute-done((f32[8,128]{1,0:T(8,128)S(1)}, f32[8,128]{1,0:T(8,128)S(1)}, u32[]{:S(2)}, u32[]{:S(2)}) %collective-permute-start) | collective-permute-done | bytes 4128 | tf_op jit(solution)/shard_map/ppermute | solution.py:303
  54.0 0.3 collective-permute-done.1.far_ref
  54.3 0.4 bin.1
  54.7 12.8 %all_to_all.22.parts_ref = f32[32,8,128]{2,1,0:T(8,128)S(1)} all-to-all(f32[32,8,128]{2,1,0:T(8,128)S(1)} %bitcast.14), channel_id=1, replica_groups=mesh['z'=8,'y'=4,'x'=4,'c'=2] {'y','x','c'}, dimensions={0} | all-to-all | bytes 262144 | tf_op jit(solution)/shard_map/all_to_all | solution.py:311
  67.6 12.3 %all_to_all.23 = f32[32,8,128]{2,1,0:T(8,128)S(1)} all-to-all(f32[32,8,128]{2,1,0:T(8,128)S(1)} %fold.1), channel_id=1, replica_groups=mesh['z'=8,'y'=4,'x'=4,'c'=2] {'z','y'}, dimensions={0} | all-to-all | bytes 262144 | tf_op jit(solution)/shard_map/all_to_all | solution.py:315
  79.9 0.6 bitcast_reduce_fusion
  (2 shorter events, 0.1 us)
Async XLA Ops:
  0.0 38.5 %copy-start = (f32[1024,512]{1,0:T(8,128)S(1)}, f32[1024,512]{1,0:T(8,128)}, u32[]{:S(2)}) copy-start(f32[1024,512]{1,0:T(8,128)} %templates_ref.1) | copy-start | bytes 6291460
  3.1 48.4 %copy-start.1 = (s32[1024,256]{1,0:T(8,128)S(1)}, s32[1024,256]{1,0:T(8,128)}, u32[]{:S(2)}) copy-start(s32[1024,256]{1,0:T(8,128)} %index_ref) | copy-start | bytes 3145732
  3.1 48.4 %copy-start.2 = (s32[256]{0:T(256)S(1)}, s32[256]{0:T(256)}, u32[]{:S(2)}) copy-start(s32[256]{0:T(256)} %param.17) | copy-start | bytes 3076
  50.3 3.8 %collective-permute-start = (f32[8,128]{1,0:T(8,128)S(1)}, f32[8,128]{1,0:T(8,128)S(1)}, u32[]{:S(2)}, u32[]{:S(2)}) collective-permute-start(f32[8,128]{1,0:T(8,128)S(1)} %get-tuple-element.28), channel_id=1, source_target_pairs={{0,24},{8,16},{16,8},{24,0},{1,25},{9,17},{17,9},{25,1},{2,26},{10... | collective-permute-start | bytes 12296 | tf_op jit(solution)/shard_map/ppermute | solution.py:303
  50.7 3.7 %collective-permute-start.1 = (f32[8,128]{1,0:T(8,128)S(1)}, f32[8,128]{1,0:T(8,128)S(1)}, u32[]{:S(2)}, u32[]{:S(2)}) collective-permute-start(f32[8,128]{1,0:T(8,128)S(1)} %get-tuple-element.29), channel_id=1, source_target_pairs={{0,224},{8,232},{16,48},{24,56},{32,64},{40,72},{48,16},{56,24},{6... | collective-permute-start | bytes 12296 | tf_op jit(solution)/shard_map/ppermute | solution.py:304

commit v9 on v8

--- a/solution.py
+++ b/solution.py
@@ -312,7 +312,10 @@
         partial.reshape(32, 8, SEGLEN), ("y", "x", "c"), split_axis=0, concat_axis=0, tiled=True
     )
     copies = call(fold_kernel, [VMEM], [((32, 8, SEGLEN), f32)], "fold")(spread)
-    sums = lax.all_to_all(copies, ("z", "y"), split_axis=0, concat_axis=0, tiled=True)
+    spread_planes = [[4 * z + y for z in (0, 4, 2, 6, 1, 5, 3, 7) for y in range(4)]]
+    sums = lax.all_to_all(
+        copies, ("z", "y"), split_axis=0, concat_axis=0, axis_index_groups=spread_planes, tiled=True
+    )
     return jnp.sum(sums.reshape(8, 32, SEGLEN), axis=0)
 
 

time: 80.7 us -> 81 us (level)
  no operation moved by 1% of the time
where the time goes in v9:
time: 81 us; the launch traced here: 80.8 us
  blocking collectives  71.2 us (88%)
  Pallas kernels  5.29 us (7%)
  waiting for transfers between devices  2.39 us (3%)
  starting transfers between devices  1.2 us (1%)
    all_to_all x1, blocking collectives, local(): lax.all_to_all(weighted.reshape(SEGMENTS, OWN_DETS, SEGLEN), ALL, split_a...  35.4 us
    all_to_all x1, blocking collectives, local(): lax.all_to_all(partial.reshape(32, 8, SEGLEN), ('y', 'x', 'c'), split_axi...  12.8 us
    all_to_all x1, blocking collectives, local(): lax.all_to_all(copies, ('z', 'y'), split_axis=0, concat_axis=0, axis_inde...  12.6 us
    all_to_all x1, blocking collectives, local(): lax.all_to_all(power, ('y', 'x', 'c'), split_axis=0, concat_axis=0, axis_...  10.4 us
    pallas_call x1, Pallas kernels, local(): call(weight_kernel, [HBM] * 7, [((DETS, SEGLEN), f32), lines, lines, line...  3.1 us
    ppermute x1, waiting for transfers between devices, local(): near = lax.ppermute(near, 'y', [(i, 3 - i) for i in range(4)])  2.08 us
  transfers between devices with their start and end apart: 2, of which 2 were waited for; matrix products, arithmetic and copies ran while one was open for 0% of the time, Pallas kernels for 1%

profile of v9, /device:TPU:1, one launch (start us, length us, event | category | flops | bytes accessed | tf_op | source)
XLA Modules:
  0.0 80.8 jit_solution(1249819120566926024)
XLA Ops:
  0.0 0.0 copy-start
  0.0 3.1 %weight.1 = (f32[1024,128]{1,0:T(8,128)S(1)}, f32[16,8,128]{2,1,0:T(8,128)S(1)}, f32[16,8,128]{2,1,0:T(8,128)S(1)}, f32[16,8,128]{2,1,0:T(8,128)S(1)}, f32[2,8,128]{2,1,0:T(8,128)S(1)}) custom-call(s32[33]{0:T(128)} %bounds_hbm.1, f32[4]{0:T(128)} %knee_hbm.1, f32[4]{0:T(128)} %slope_hbm.1, f32[4]{0:T(128)} %level_hbm.1, f32[1024,128]{1,0:T(8,128)} %bitcast.17, ...), custom_call_target="tpu_custom_call" | custom-call | tf_op jit(solution)/shard_map/weight/pallas_call | solution.py:290
  3.1 0.0 copy-start.1
  3.1 0.0 copy-start.2
  3.1 35.4 %all_to_all.20 = f32[256,4,128]{2,1,0:T(4,128)S(1)} all-to-all(f32[256,4,128]{2,1,0:T(4,128)S(1)} %bitcast.15), channel_id=1, replica_groups=mesh['z'=8,'y'=4,'x'=4,'c'=2] {'z','y','x','c'}, dimensions={0} | all-to-all | bytes 1048576 | tf_op jit(solution)/shard_map/all_to_all | solution.py:293
  38.5 0.0 copy-done
  38.5 1.3 %project.1 = (f32[128,1024]{1,0:T(8,128)S(1)}, f32[16,8,128]{2,1,0:T(8,128)S(1)}) custom-call(f32[1024,128]{1,0:T(8,128)S(1)} %bitcast.13, f32[1024,512]{1,0:T(8,128)S(1)} %copy-done), custom_call_target="tpu_custom_call" | custom-call | tf_op jit(solution)/shard_map/project/pallas_call | solution.py:296
  39.8 10.4 %all_to_all.21.gathered_ref = f32[16,8,128]{2,1,0:T(8,128)S(1)} all-to-all(f32[16,8,128]{2,1,0:T(8,128)S(1)} %get-tuple-element.20), channel_id=1, replica_groups={{0,1,2,3,4,5,6,7,8,9,10,11,12,13,14,15},{16,17,18,19,20,21,22,23,24,25,..., dimensions={0} | all-to-all | bytes 131072 | tf_op jit(solution)/shard_map/all_to_all | solution.py:297
  50.3 0.4 collective-permute-start
  50.7 0.8 collective-permute-start.1
  51.5 0.0 copy-done.1
  51.5 0.0 copy-done.2
  51.5 0.5 slots.1.hot_ref
  51.9 2.1 %collective-permute-done.near_ref = f32[8,128]{1,0:T(8,128)S(1)} collective-permute-done((f32[8,128]{1,0:T(8,128)S(1)}, f32[8,128]{1,0:T(8,128)S(1)}, u32[]{:S(2)}, u32[]{:S(2)}) %collective-permute-start) | collective-permute-done | bytes 4128 | tf_op jit(solution)/shard_map/ppermute | solution.py:303
  54.0 0.3 collective-permute-done.1.far_ref
  54.3 0.4 bin.1
  54.7 12.8 %all_to_all.22.parts_ref = f32[32,8,128]{2,1,0:T(8,128)S(1)} all-to-all(f32[32,8,128]{2,1,0:T(8,128)S(1)} %bitcast.14), channel_id=1, replica_groups=mesh['z'=8,'y'=4,'x'=4,'c'=2] {'y','x','c'}, dimensions={0} | all-to-all | bytes 262144 | tf_op jit(solution)/shard_map/all_to_all | solution.py:311
  67.6 12.6 %all_to_all.23 = f32[32,8,128]{2,1,0:T(8,128)S(1)} all-to-all(f32[32,8,128]{2,1,0:T(8,128)S(1)} %fold.1), channel_id=1, replica_groups={{0,8,16,24,128,136,144,152,64,72,80,88,192,200,208,216,32,40,48,56,160,..., dimensions={0} | all-to-all | bytes 262144 | tf_op jit(solution)/shard_map/all_to_all | solution.py:316
  80.2 0.6 bitcast_reduce_fusion
  (2 shorter events, 0.1 us)
Async XLA Ops:
  0.0 38.5 %copy-start = (f32[1024,512]{1,0:T(8,128)S(1)}, f32[1024,512]{1,0:T(8,128)}, u32[]{:S(2)}) copy-start(f32[1024,512]{1,0:T(8,128)} %templates_ref.1) | copy-start | bytes 6291460
  3.1 48.4 %copy-start.1 = (s32[1024,256]{1,0:T(8,128)S(1)}, s32[1024,256]{1,0:T(8,128)}, u32[]{:S(2)}) copy-start(s32[1024,256]{1,0:T(8,128)} %index_ref) | copy-start | bytes 3145732
  3.1 48.4 %copy-start.2 = (s32[256]{0:T(256)S(1)}, s32[256]{0:T(256)}, u32[]{:S(2)}) copy-start(s32[256]{0:T(256)} %param.17) | copy-start | bytes 3076
  50.3 3.8 %collective-permute-start = (f32[8,128]{1,0:T(8,128)S(1)}, f32[8,128]{1,0:T(8,128)S(1)}, u32[]{:S(2)}, u32[]{:S(2)}) collective-permute-start(f32[8,128]{1,0:T(8,128)S(1)} %get-tuple-element.28), channel_id=1, source_target_pairs={{0,24},{8,16},{16,8},{24,0},{1,25},{9,17},{17,9},{25,1},{2,26},{10... | collective-permute-start | bytes 12296 | tf_op jit(solution)/shard_map/ppermute | solution.py:303
  50.7 3.7 %collective-permute-start.1 = (f32[8,128]{1,0:T(8,128)S(1)}, f32[8,128]{1,0:T(8,128)S(1)}, u32[]{:S(2)}, u32[]{:S(2)}) collective-permute-start(f32[8,128]{1,0:T(8,128)S(1)} %get-tuple-element.29), channel_id=1, source_target_pairs={{0,224},{8,232},{16,48},{24,56},{32,64},{40,72},{48,16},{56,24},{6... | collective-permute-start | bytes 12296 | tf_op jit(solution)/shard_map/ppermute | solution.py:304
